TPU v7x, 512 devices: a whole 4x4x16 slice. The times are simulated.
512 devices in a mesh: tm: 32 (over x, y, z_hi), chan: 16 (over z_lo, core).
Axes of the slice: x: 4, y: 4, z: 16 (z_hi: 2, z_lo: 8; z = z_hi * 8 + z_lo), core: 2. Of those that a mesh axis runs over, the one named last changes fastest.
Arguments:
- waveform: bfloat16 [32768, 10240], P('tm', 'chan'), may hold values from -750 to 750
- templates: bfloat16 [16, 256, 10240], P(None, 'tm', 'chan'), may hold values from -40 to 40
Outputs:
- detection: float32 [16, 32768], P(None, ('tm', 'chan'))
All inputs are finite; a program needn't handle non-finite values.
Results may differ from a plain program's by a relative error of at most 0.0003.
Values may be sent and summed in bfloat16 or wider, within the bound.
No kernel may reach another device: no remote copies, remote signals or barrier semaphores. Data moves between devices by JAX's collectives and lax.ppermute only.
A program may use at most 128 MiB of HBM per device.

v0:
```python
import math

import jax
import jax.numpy as jnp
from jax import lax
from jax.sharding import PartitionSpec as P

CH = 10240
L = 256
K = 16


def passed_along(block, axis, distance):
    devices = range(lax.axis_size(axis))
    route = [(i - distance, i) for i in devices if i - distance in devices]
    return lax.ppermute(block, axis, route)


def correlate(partial_value, shard_lags, padded, sample_rows):
    padded_rows = padded.shape[0]
    chan_width = padded.shape[1]
    lag_count = shard_lags.shape[1]
    group_size = math.gcd(lag_count, 32)

    def one_group(group_index, running):
        lag_block = lax.dynamic_slice_in_dim(shard_lags, group_index * group_size, group_size, 1)
        flat_block = lag_block.reshape(K * group_size, chan_width)
        products = lax.dot_general(
            flat_block, padded, (((1,), (1,)), ((), ())), preferred_element_type=jnp.float32
        )
        products = products.reshape(K, group_size * padded_rows)
        products = jnp.pad(products, ((0, 0), (0, group_size)))
        products = products.reshape(K, group_size, padded_rows + 1)
        window = lax.dynamic_slice_in_dim(products, group_index * group_size, sample_rows, 2)
        return running + jnp.sum(window, axis=1)

    return lax.fori_loop(0, lag_count // group_size, one_group, partial_value)


def local(waveform, templates):
    sample_rows = waveform.shape[0]
    norm_scale = math.sqrt(L * CH)
    next_rim = passed_along(waveform[: L - 1], "tm", -1)
    padded = jnp.concatenate([waveform, next_rim], axis=0)
    shard_lags = lax.all_gather(templates, "tm", axis=1, tiled=True)
    running = jnp.zeros((K, sample_rows), jnp.float32)
    running = correlate(running, shard_lags, padded, sample_rows)
    lag_values = shard_lags.astype(jnp.float32)
    energy = jnp.sum(lag_values * lag_values, axis=(1, 2))
    stack = running
    template_energy = energy
    squares = jnp.sum(jnp.square(padded.astype(jnp.float32)), axis=1)
    data_energy = lax.reduce_window(squares, jnp.float32(0.0), lax.add, (L,), (1,), "VALID")
    share_rows = sample_rows // lax.axis_size("chan")
    stack, data_energy, template_energy = lax.psum((stack, data_energy, template_energy), "chan")
    offset = lax.axis_index("chan") * share_rows
    stack = lax.dynamic_slice_in_dim(stack, offset, share_rows, 1)
    data_energy = lax.dynamic_slice_in_dim(data_energy, offset, share_rows, 0)
    return (
        stack
        * norm_scale
        * lax.rsqrt(data_energy + 1e-06)[None, :]
        * lax.rsqrt(template_energy)[:, None]
    )


def solution(mesh):
    in_specs = (P("tm", "chan"), P(None, "tm", "chan"))
    out_specs = P(None, ("tm", "chan"))
    return jax.shard_map(local, mesh=mesh, in_specs=in_specs, out_specs=out_specs, check_vma=False)
```

profile of v0, /device:TPU:1, one launch (start us, length us, event | category | flops | bytes accessed | tf_op | source)
XLA Modules:
  0.0 498.8 jit_solution(1364822901660622940)
XLA Ops:
  6.5 0.7 all-gather.2.cloned.1.call-update
  7.3 1.0 slice.3
  8.3 1.3 collective-permute-start
  9.6 2.6 constant_dynamic-update-slice_fusion.1
  12.2 17.4 %collective-permute-done = bf16[255,640]{1,0:T(8,128)(2,1)S(1)} collective-permute-done((bf16[255,640]{1,0:T(8,128)(2,1)S(1)}, bf16[255,640]{1,0:T(8,128)(2,1)S(1)}, u32[]{:S(2)}, u32[]{:S(2)}) %collective-permute-start) | collective-permute-done | bytes 326432 | tf_op jit(solution)/shard_map/ppermute | solution.py:16
  29.6 0.8 constant_dynamic-update-slice_fusion
  30.4 1.8 multiply_reduce_fusion.1
  32.2 0.2 reshape.63
  32.5 35.4 %reduce-window.9 = f32[1024,1]{1,0:T(8,128)S(1)} reduce-window(f32[1279,1]{1,0:T(8,128)S(1)} %reshape.63, f32[]{:T(128)} %constant.74.clone.1), window={size=256x1}, to_apply=%region_5.6 | reduce-window | flops 261120 | bytes 9216 | tf_op jit(solution)/shard_map/reduce-window.4
  67.8 0.2 reduce
  68.1 169.2 %all-gather.2.cloned.1.call-done = bf16[16,256,640]{2,1,0:T(8,128)(2,1)} async-done(((bf16[16,8,640]{2,1,0:T(8,128)(2,1)}), bf16[16,256,640]{2,1,0:T(8,128)(2,1)}) %all-gather.2.cloned.1.call-update) | async-done | bytes 5242896 | tf_op jit(solution)/shard_map/all_gather | solution.py:45
  237.3 78.4 %while.16 = (s32[]{:T(128)}, f32[16,1024]{1,0:T(8,128)S(1)}, bf16[16,256,640]{2,1,0:T(8,128)(2,1)}, bf16[1279,640]{1,0:T(8,128)(2,1)}, s32[]{:T(128)}, /*index=5...) while((s32[]{:T(128)}, f32[16,1024]{1,0:T(8,128)S(1)}, bf16[16,256,640]{2,1,0:T(8,128)(2,1)}, ...), condition=%wide.region_2.3_spmd.clone, body=%wide.region_0.2_spmd.clone.sunk | while | flops 838746112 | bytes 24304584 | solution.py:37
  237.3 1.1 constant_dynamic-slice_fusion.2
  238.4 4.2 fusion.8
  242.6 2.8 reshape.66
  245.4 0.2 pad.13
  245.5 0.8 copy.6
  246.3 0.6 dynamic-slice_reduce_fusion.2
  247.0 1.2 constant_dynamic-slice_fusion.2
  248.2 4.2 fusion.8
  252.4 2.8 reshape.66
  255.2 0.2 pad.13
  255.3 0.8 copy.6
  256.1 0.6 dynamic-slice_reduce_fusion.2
  256.8 1.2 constant_dynamic-slice_fusion.2
  258.0 4.2 fusion.8
  262.2 2.8 reshape.66
  264.9 0.2 pad.13
  265.1 0.8 copy.6
  265.9 0.6 dynamic-slice_reduce_fusion.2
  266.6 1.2 constant_dynamic-slice_fusion.2
  267.8 4.2 fusion.8
  271.9 2.8 reshape.66
  274.7 0.2 pad.13
  274.9 0.8 copy.6
  275.7 0.6 dynamic-slice_reduce_fusion.2
  276.4 1.2 constant_dynamic-slice_fusion.2
  277.6 4.2 fusion.8
  281.7 2.8 reshape.66
  284.5 0.2 pad.13
  284.7 0.8 copy.6
  285.5 0.7 dynamic-slice_reduce_fusion.2
  286.2 1.2 constant_dynamic-slice_fusion.2
  287.4 4.2 fusion.8
  291.5 2.8 reshape.66
  294.3 0.2 pad.13
  294.5 0.8 copy.6
  295.3 0.7 dynamic-slice_reduce_fusion.2
  296.0 1.2 constant_dynamic-slice_fusion.2
  297.2 4.2 fusion.8
  301.4 2.8 reshape.66
  304.2 0.2 pad.13
  304.3 0.8 copy.6
  305.1 0.7 dynamic-slice_reduce_fusion.2
  305.9 1.2 constant_dynamic-slice_fusion.2
  307.0 4.2 fusion.8
  311.2 2.8 reshape.66
  314.2 0.8 copy.6
  314.9 0.7 dynamic-slice_reduce_fusion.2
  315.7 0.6 copy-done
  316.3 3.7 multiply_reduce_fusion
  320.0 46.5 %all-reduce.1 = (f32[16]{0:T(128)S(1)}, f32[1024]{0:T(1024)S(1)}) all-reduce(f32[16]{0:T(128)S(1)} %multiply_reduce_fusion, f32[1024]{0:T(1024)S(1)} %reduce), channel_id=1, replica_groups=mesh['tm'=32,'chan'=16] {'chan'}, use_global_device_ids=true, to_apply=%region_8.9 | all-reduce | flops 1040 | bytes 8320 | tf_op jit(solution)/shard_map/psum | solution.py:55
  366.5 123.8 %all-reduce.4.cloned.1.call-done = f32[16,1024]{1,0:T(8,128)} async-done(((f32[16,1024]{1,0:T(8,128)}), f32[16,1024]{1,0:T(8,128)}) %all-reduce.4.cloned.1.call-update) | async-done | bytes 65552 | tf_op jit(solution)/shard_map/psum | solution.py:55
  490.4 1.4 multiply_multiply_fusion
  (16 shorter events, 0.5 us)
Async XLA Ops:
  6.5 230.7 %all-gather.2.cloned.1.call-start = ((), (), s32[]{:S(2)}) async-start(), calls=%async_computation | async-start | bytes 5406720 | tf_op jit(solution)/shard_map/all_gather | solution.py:45
  7.3 483.1 %all-reduce.4.cloned.1.call-start = ((), (), s32[]{:S(2)}) async-start(), calls=%async_computation.1 | async-start | bytes 131072 | tf_op jit(solution)/shard_map/psum | solution.py:55
  8.3 21.3 %collective-permute-start = (bf16[255,640]{1,0:T(8,128)(2,1)S(1)}, bf16[255,640]{1,0:T(8,128)(2,1)S(1)}, u32[]{:S(2)}, u32[]{:S(2)}) collective-permute-start(bf16[255,640]{1,0:T(8,128)(2,1)S(1)} %slice.3), channel_id=1, source_target_pairs={{16,0},{32,16},{48,32},{64,48},{80,64},{96,80},{112,96},{128,112},... | collective-permute-start | bytes 979208 | tf_op jit(solution)/shard_map/ppermute | solution.py:16
  315.7 0.6 copy-start
Sparse Core Ops, SparseCore 0:
  11.5 225.7 all-gather.1
  316.4 173.8 all-reduce.3
where the time goes:
time: 509 us; the launch traced here: 499 us
  waiting for transfers between devices  311 us (61%)
  other arithmetic  47.9 us (9%)
  blocking collectives  46.5 us (9%)
  local copies, waits for them, and re-layouts  44.3 us (9%)
  matrix products  33.3 us (7%)
  between operations  13.7 us (3%)
    all_gather x1, waiting for transfers between devices, local(): shard_lags = lax.all_gather(templates, 'tm', axis=1, tiled=True)  169 us
    psum x1, waiting for transfers between devices, local(): lax.psum((stack, data_energy, template_energy), 'chan')  124 us
    psum x1, blocking collectives, local(): lax.psum((stack, data_energy, template_energy), 'chan')  46.5 us
    another operation x2, other arithmetic  35.6 us
    dot_general x8, matrix products, one_group(): lax.dot_general(flat_block, padded, (((1,), (1,)), ((), ())), preferred_e...  33.3 us
    reshape x8, local copies, waits for them, and re-layouts, one_group(): products = products.reshape(K, group_size * padded_rows)  22.3 us
    ppermute x1, waiting for transfers between devices, passed_along(): return lax.ppermute(block, axis, route)  17.4 us
  transfers between devices with their start and end apart: 3, of which 3 were waited for; matrix products, arithmetic and copies ran while one was open for 9% of the time, Pallas kernels for 0%

commit v1 on v0

v1 whole, which is shorter than its diff:
```python
import math

import jax
import jax.numpy as jnp
from jax import lax
from jax.experimental import pallas as pl
from jax.experimental.pallas import tpu as pltpu
from jax.sharding import PartitionSpec as P

CH = 10240
L = 256
K = 16
SUB = 8
ROWS = 1024
RIM = 256
SPAN = ROWS + 128
NT = (((1,), (1,)), ((), ()))


def correlate_kernel(z_ref, x_ref, rim_ref, own_ref, oth_ref, out_ref, xs, q):
    xs[0:ROWS] = x_ref[...]
    xs[ROWS : ROWS + RIM] = rim_ref[...]
    used = ROWS + 16

    def step(i, te):
        w = jnp.concatenate([own_ref[i], oth_ref[i]], axis=0)
        rows = pl.ds(pl.multiple_of(16 * i, 16), used)
        part = lax.dot_general(xs[rows, :], w, NT, preferred_element_type=jnp.float32)
        q[0:used, :] = jnp.where(i == 0, part, q[0:used, :] + part)
        wf = w.astype(jnp.float32)
        sq = wf * wf
        for j in range(5):
            te = te + sq[:, 128 * j : 128 * j + 128]
        return te

    te = lax.fori_loop(0, 16, step, jnp.zeros((2 * K * SUB, 128), jnp.float32))
    te = jnp.sum(te.reshape(2, K, SUB, 128), axis=(0, 2))
    te = jnp.sum(te, axis=1, keepdims=True)

    q[used:SPAN, :] = jnp.zeros((SPAN - used, 2 * K * SUB), jnp.float32)
    halves = []
    for h in range(2):
        p = jnp.transpose(q[:, 128 * h : 128 * h + 128])
        p = p.reshape(K, SUB, SPAN)
        lag = lax.broadcasted_iota(jnp.int32, (K, SUB, SPAN), 1)
        for b in (1, 2, 4):
            p = jnp.where((lag & b) != 0, pltpu.roll(p, SPAN - b, 2), p)
        halves.append(jnp.sum(p, axis=1))
    shift = [pltpu.roll(p, SPAN - SUB, 1) for p in halves]
    upper = z_ref[0] == 1
    stack = jnp.where(upper, shift[0] + halves[1], halves[0] + shift[1])

    sq = jnp.zeros((ROWS + RIM, 128), jnp.float32)
    for j in range(5):
        v = xs[:, 128 * j : 128 * j + 128].astype(jnp.float32)
        sq = sq + v * v
    de = jnp.sum(jnp.transpose(sq), axis=0, keepdims=True)
    de = jnp.broadcast_to(de, (8, ROWS + RIM))
    for b in range(8):
        de = de + pltpu.roll(de, ROWS + RIM - (1 << b), 1)

    lane = lax.broadcasted_iota(jnp.int32, (8, 128), 1)
    te_row = jnp.where(lane < 96, te[0:8], te[8:16])
    for d in range(16):
        tile = slice(128 * (d // 2), 128 * (d // 2) + 128)
        lo, hi, en = stack[0:8, tile], stack[8:16, tile], de[:, tile]
        if d % 2 == 0:
            hi = pltpu.roll(hi, 64, 1)
        else:
            lo, en = pltpu.roll(lo, 64, 1), pltpu.roll(en, 64, 1)
        out_ref[d, 0:8, :] = jnp.where(lane < 64, lo, hi)
        out_ref[d, 8:16, :] = jnp.where(lane < 64, en, te_row)


def correlate(z, x, rim, own, oth):
    vmem = pl.BlockSpec(memory_space=pltpu.VMEM)
    return pl.pallas_call(
        correlate_kernel,
        out_shape=jax.ShapeDtypeStruct((16, 16, 128), jnp.float32),
        in_specs=[pl.BlockSpec(memory_space=pltpu.SMEM), vmem, vmem, vmem, vmem],
        out_specs=vmem,
        scratch_shapes=[
            pltpu.VMEM((ROWS + RIM, 640), jnp.bfloat16),
            pltpu.VMEM((SPAN, 2 * K * SUB), jnp.float32),
        ],
        compiler_params=pltpu.CompilerParams(vmem_limit_bytes=40 * 2**20),
        cost_estimate=pl.CostEstimate(flops=5_500_000_000, bytes_accessed=7_000_000, transcendentals=0),
        name="correlate",
    )(z, x, rim, own, oth)


def finish_kernel(parts_ref, out_ref):
    total = jnp.sum(parts_ref[...], axis=0)
    scale = math.sqrt(L * CH)
    rows, energies = total[0:8], total[8:16]
    inv = lax.rsqrt(energies[:, 0:64] + 1e-06) * scale
    out_ref[0:8, :] = rows[:, 0:64] * inv * lax.rsqrt(energies[:, 64:65])
    out_ref[8:16, :] = rows[:, 64:128] * inv * lax.rsqrt(energies[:, 96:97])


def finish(parts):
    vmem = pl.BlockSpec(memory_space=pltpu.VMEM)
    return pl.pallas_call(
        finish_kernel,
        out_shape=jax.ShapeDtypeStruct((K, 64), jnp.float32),
        in_specs=[vmem],
        out_specs=vmem,
        name="finish",
    )(parts)


def local(waveform, templates):
    tm = lax.axis_size("tm")
    z = lax.rem(lax.axis_index("tm"), 2)
    plane = [[2 * i + h for i in range(tm // 2)] for h in range(2)]
    shard = templates.reshape(K * SUB, -1)
    other = lax.ppermute(shard, "tm", [(i, i ^ 1) for i in range(tm)])
    rim = lax.ppermute(waveform[:RIM], "tm", [(i, i - 1) for i in range(1, tm)])

    def spread(block):
        copies = jnp.broadcast_to(block[None], (tm // 2,) + block.shape)
        return lax.all_to_all(copies, "tm", 0, 0, axis_index_groups=plane)

    own_all = spread(shard)
    oth_all = spread(other)
    parts = correlate(z.reshape(1), waveform, rim, own_all, oth_all)
    parts = lax.all_to_all(parts, "chan", 0, 0)
    return finish(parts)


def solution(mesh):
    in_specs = (P("tm", "chan"), P(None, "tm", "chan"))
    out_specs = P(None, ("tm", "chan"))
    return jax.shard_map(local, mesh=mesh, in_specs=in_specs, out_specs=out_specs, check_vma=False)
```

time: 509 us -> 140 us (0.28)
  the two profiles are of different devices: /device:TPU:1 before, /device:TPU:13 now
where the time goes in v1:
time: 140 us
  starting transfers between devices  46.9 us (34%)
  blocking collectives  44.6 us (32%)
  waiting for transfers between devices  25.5 us (18%)
  Pallas kernels  15.7 us (11%)
  local copies, waits for them, and re-layouts  6.88 us (5%)
    all_to_all x1, blocking collectives, local(): parts = lax.all_to_all(parts, 'chan', 0, 0)  44.6 us
    ppermute x1, starting transfers between devices, local(): rim = lax.ppermute(waveform[:RIM], 'tm', [(i, i - 1) for i in range(1, tm)])  17.3 us
    all_to_all x2, waiting for transfers between devices, spread(): return lax.all_to_all(copies, 'tm', 0, 0, axis_index_groups=plane)  17.2 us
    ppermute x1, starting transfers between devices, local(): other = lax.ppermute(shard, 'tm', [(i, i ^ 1) for i in range(tm)])  15.4 us
    all_to_all x2, starting transfers between devices, spread(): return lax.all_to_all(copies, 'tm', 0, 0, axis_index_groups=plane)  14.1 us
    pallas_call x1, Pallas kernels, correlate(): pl.pallas_call(correlate_kernel, out_shape=jax.ShapeDtypeStruct((16, 16,...  14 us
    ppermute x1, waiting for transfers between devices, local(): rim = lax.ppermute(waveform[:RIM], 'tm', [(i, i - 1) for i in range(1, tm)])  5.08 us
    broadcast_in_dim x2, local copies, waits for them, and re-layouts, spread(): copies = jnp.broadcast_to(block[None], (tm // 2,) + block.shape)  4.56 us
  transfers between devices with their start and end apart: 4, of which 4 were waited for; matrix products, arithmetic and copies ran while one was open for 1% of the time, Pallas kernels for 0%

profile of v1, /device:TPU:13, one launch (start us, length us, event | category | flops | bytes accessed | tf_op | source)
XLA Modules:
  0.0 139.5 jit_solution(14408768469354877124)
XLA Ops:
  0.0 2.7 %broadcast_in_dim.14 = bf16[16,128,640]{2,1,0:T(8,128)(2,1)} broadcast(bf16[128,640]{1,0:T(8,128)(2,1)} %bitcast.2), dimensions={1,2} | broadcast | bytes 2785280 | tf_op jit(solution)/shard_map/broadcast_in_dim | solution.py:121
  2.7 0.0 copy-start.1
  2.7 6.9 %all-to-all-start = ((bf16[16,128,640]{2,1,0:T(8,128)(2,1)}), bf16[16,128,640]{2,1,0:T(8,128)(2,1)S(1)}, u32[]{:S(2)}, u32[]{:S(2)}) async-start(bf16[16,128,640]{2,1,0:T(8,128)(2,1)} %broadcast_in_dim.14), calls=%async_computation | async-start | bytes 5242880 | tf_op jit(solution)/shard_map/all_to_all | solution.py:122
  9.7 0.0 copy-done.1
  9.7 15.4 %collective-permute-start.1 = (bf16[128,640]{1,0:T(8,128)(2,1)S(1)}, bf16[128,640]{1,0:T(8,128)(2,1)S(1)}, u32[]{:S(2)}, u32[]{:S(2)}) collective-permute-start(bf16[128,640]{1,0:T(8,128)(2,1)S(1)} %bitcast.3), channel_id=1, source_target_pairs={{0,16},{16,0},{32,48},{48,32},{64,80},{80,64},{96,112},{112,96},{1... | collective-permute-start | bytes 491528 | tf_op jit(solution)/shard_map/ppermute | solution.py:117
  25.1 3.3 %collective-permute-done.1 = bf16[128,640]{1,0:T(8,128)(2,1)S(1)} collective-permute-done((bf16[128,640]{1,0:T(8,128)(2,1)S(1)}, bf16[128,640]{1,0:T(8,128)(2,1)S(1)}, u32[]{:S(2)}, u32[]{:S(2)}) %collective-permute-start.1) | collective-permute-done | bytes 163872 | tf_op jit(solution)/shard_map/ppermute | solution.py:117
  28.4 11.9 %all-to-all-done.own_ref = bf16[16,128,640]{2,1,0:T(8,128)(2,1)S(1)} async-done(((bf16[16,128,640]{2,1,0:T(8,128)(2,1)}), bf16[16,128,640]{2,1,0:T(8,128)(2,1)S(1)}, u32[]{:S(2)}, u32[]{:S(2)}) %all-to-all-start) | async-done | bytes 2621472 | tf_op jit(solution)/shard_map/all_to_all | solution.py:122
  40.3 1.8 %broadcast_in_dim.15 = bf16[16,128,640]{2,1,0:T(8,128)(2,1)} broadcast(bf16[128,640]{1,0:T(8,128)(2,1)S(1)} %collective-permute-done.1), dimensions={1,2} | broadcast | bytes 2785280 | tf_op jit(solution)/shard_map/broadcast_in_dim | solution.py:121
  42.1 7.2 %all-to-all-start.1 = ((bf16[16,128,640]{2,1,0:T(8,128)(2,1)}), bf16[16,128,640]{2,1,0:T(8,128)(2,1)}, u32[]{:S(2)}, u32[]{:S(2)}) async-start(bf16[16,128,640]{2,1,0:T(8,128)(2,1)} %broadcast_in_dim.15), calls=%async_computation.1 | async-start | bytes 5242880 | tf_op jit(solution)/shard_map/all_to_all | solution.py:122
  49.4 1.0 slice.3
  50.4 17.3 %collective-permute-start = (bf16[256,640]{1,0:T(8,128)(2,1)S(1)}, bf16[256,640]{1,0:T(8,128)(2,1)S(1)}, u32[]{:S(2)}, u32[]{:S(2)}) collective-permute-start(bf16[256,640]{1,0:T(8,128)(2,1)S(1)} %slice.3), channel_id=1, source_target_pairs={{16,0},{32,16},{48,32},{64,48},{80,64},{96,80},{112,96},{128,112},... | collective-permute-start | bytes 983048 | tf_op jit(solution)/shard_map/ppermute | solution.py:118
  67.6 5.1 %collective-permute-done.rim_ref = bf16[256,640]{1,0:T(8,128)(2,1)S(1)} collective-permute-done((bf16[256,640]{1,0:T(8,128)(2,1)S(1)}, bf16[256,640]{1,0:T(8,128)(2,1)S(1)}, u32[]{:S(2)}, u32[]{:S(2)}) %collective-permute-start) | collective-permute-done | bytes 327712 | tf_op jit(solution)/shard_map/ppermute | solution.py:118
  72.7 5.3 %all-to-all-done.1.oth_ref = bf16[16,128,640]{2,1,0:T(8,128)(2,1)} async-done(((bf16[16,128,640]{2,1,0:T(8,128)(2,1)}), bf16[16,128,640]{2,1,0:T(8,128)(2,1)}, u32[]{:S(2)}, u32[]{:S(2)}) %all-to-all-start.1) | async-done | bytes 2621472 | tf_op jit(solution)/shard_map/all_to_all | solution.py:122
  78.0 0.0 copy-start
  78.0 1.3 copy-done
  79.3 14.0 %correlate.1 = f32[16,16,128]{2,1,0:T(8,128)S(1)} custom-call(s32[1]{0:T(128)} %bitcast.z_ref, bf16[1024,640]{1,0:T(8,128)(2,1)S(1)} %copy-done, bf16[256,640]{1,0:T(8,128)(2,1)S(1)} %collective-permute-done.rim_ref, bf16[16,128,640]{2,1,0:T(8,128)(2,1)S(1)} %all-to-all-done.own_ref, bf16[16,128,640]{2,1,0:T(8,128)(2,1)} %all-to-all-done.1.oth_ref), custom_call_target="tpu_custom_call" | custom-call | flops 5500000256 | bytes 7000000 | tf_op jit(solution)/shard_map/correlate/pallas_call | solution.py:77
  93.3 44.6 %all_to_all.15.parts_ref = f32[16,16,128]{2,1,0:T(8,128)} all-to-all(f32[16,16,128]{2,1,0:T(8,128)S(1)} %correlate.1), channel_id=1, replica_groups=mesh['tm'=32,'chan'=16] {'chan'}, dimensions={0} | all-to-all | bytes 262144 | tf_op jit(solution)/shard_map/all_to_all | solution.py:127
  137.9 1.7 %finish.1 = f32[16,64]{1,0:T(8,128)} custom-call(f32[16,16,128]{2,1,0:T(8,128)} %all_to_all.15.parts_ref), custom_call_target="tpu_custom_call" | custom-call | tf_op jit(solution)/shard_map/finish/pallas_call | solution.py:103
Async XLA Ops:
  2.7 6.9 %copy-start.1 = (bf16[16,8,640]{2,1,0:T(8,128)(2,1)S(1)}, bf16[16,8,640]{2,1,0:T(8,128)(2,1)}, u32[]{:S(2)}) copy-start(bf16[16,8,640]{2,1,0:T(8,128)(2,1)} %param.3) | copy-start | bytes 491524
  2.7 37.6 %all-to-all-start = ((bf16[16,128,640]{2,1,0:T(8,128)(2,1)}), bf16[16,128,640]{2,1,0:T(8,128)(2,1)S(1)}, u32[]{:S(2)}, u32[]{:S(2)}) async-start(bf16[16,128,640]{2,1,0:T(8,128)(2,1)} %broadcast_in_dim.14), calls=%async_computation | async-start | bytes 5242880 | tf_op jit(solution)/shard_map/all_to_all | solution.py:122
  9.7 18.7 %collective-permute-start.1 = (bf16[128,640]{1,0:T(8,128)(2,1)S(1)}, bf16[128,640]{1,0:T(8,128)(2,1)S(1)}, u32[]{:S(2)}, u32[]{:S(2)}) collective-permute-start(bf16[128,640]{1,0:T(8,128)(2,1)S(1)} %bitcast.3), channel_id=1, source_target_pairs={{0,16},{16,0},{32,48},{48,32},{64,80},{80,64},{96,112},{112,96},{1... | collective-permute-start | bytes 491528 | tf_op jit(solution)/shard_map/ppermute | solution.py:117
  42.1 35.9 %all-to-all-start.1 = ((bf16[16,128,640]{2,1,0:T(8,128)(2,1)}), bf16[16,128,640]{2,1,0:T(8,128)(2,1)}, u32[]{:S(2)}, u32[]{:S(2)}) async-start(bf16[16,128,640]{2,1,0:T(8,128)(2,1)} %broadcast_in_dim.15), calls=%async_computation.1 | async-start | bytes 5242880 | tf_op jit(solution)/shard_map/all_to_all | solution.py:122
  50.4 22.4 %collective-permute-start = (bf16[256,640]{1,0:T(8,128)(2,1)S(1)}, bf16[256,640]{1,0:T(8,128)(2,1)S(1)}, u32[]{:S(2)}, u32[]{:S(2)}) collective-permute-start(bf16[256,640]{1,0:T(8,128)(2,1)S(1)} %slice.3), channel_id=1, source_target_pairs={{16,0},{32,16},{48,32},{64,48},{80,64},{96,80},{112,96},{128,112},... | collective-permute-start | bytes 983048 | tf_op jit(solution)/shard_map/ppermute | solution.py:118
  78.0 1.3 copy-start

commit v2 on v1

v2 whole, which is shorter than its diff:
```python
import math

import jax
import jax.numpy as jnp
from jax import lax
from jax.experimental import pallas as pl
from jax.experimental.pallas import tpu as pltpu
from jax.sharding import PartitionSpec as P

CH = 10240
L = 256
K = 16
SUB = 8
ROWS = 1024
RIM = 256
USED = ROWS + 16
SPAN = ROWS + 128
NN = (((1,), (0,)), ((), ()))


def swap(v):
    return jnp.concatenate([v[:, 64:], v[:, :64]], axis=1)


def low_lanes():
    return lax.broadcasted_iota(jnp.int32, (1, 128), 1) < 64


def pack_rest(v, half):
    n = v.shape[0] // 2
    if half == 0:
        return jnp.where(low_lanes(), v[:n], swap(v[n:]))
    return jnp.where(low_lanes(), swap(v[:n]), v[n:])


def pack_rows(src, n, half, keep_ref, send_ref, blank=None):
    rest = src[:, 512:640]
    first, second = pack_rest(rest, 0), pack_rest(rest, 1)
    one = half == 1
    for ref, other in ((keep_ref, False), (send_ref, True)):
        upper = jnp.logical_not(one) if other else one
        parts = [
            jnp.where(upper, src[:, 256:384], src[:, 0:128]),
            jnp.where(upper, src[:, 384:512], src[:, 128:256]),
            jnp.where(upper, second, first),
        ]
        at = 0
        for part in parts:
            if blank is not None:
                part = jnp.where(blank, jnp.zeros_like(part), part)
            ref[at : at + part.shape[0]] = part
            at += part.shape[0]


def pack_lags(src, copies_ref):
    rest = src[:, 512:640]
    for half in range(2):
        packed = jnp.concatenate(
            [src[:, 256 * half : 256 * half + 128], src[:, 256 * half + 128 : 256 * half + 256], pack_rest(rest, half)],
            axis=0,
        )
        for p in range(16):
            if (p // 4) % 2 == half:
                copies_ref[p] = packed


def first_pack_kernel(place_ref, x_ref, t_ref, keep_ref, send_ref, copies_ref):
    pack_rows(x_ref[...], ROWS, place_ref[1], keep_ref, send_ref)
    pack_lags(t_ref[...], copies_ref)


def second_pack_kernel(place_ref, c_ref, keep_ref, send_ref, copies_ref):
    pack_lags(c_ref[0:128], copies_ref)
    pack_rows(c_ref[128:384], RIM, place_ref[1], keep_ref, send_ref, blank=place_ref[2] == 1)


VMEM = pl.BlockSpec(memory_space=pltpu.VMEM)
SMEM = pl.BlockSpec(memory_space=pltpu.SMEM)


def packed(kernel, rows, name, *args):
    half = jax.ShapeDtypeStruct((rows * 5 // 2, 128), jnp.bfloat16)
    return pl.pallas_call(
        kernel,
        out_shape=(half, half, jax.ShapeDtypeStruct((16, 320, 128), jnp.bfloat16)),
        in_specs=[SMEM] + [VMEM] * (len(args) - 1),
        out_specs=(VMEM, VMEM, VMEM),
        compiler_params=pltpu.CompilerParams(vmem_limit_bytes=32 * 2**20),
        cost_estimate=pl.CostEstimate(flops=2_000_000, bytes_accessed=4_000_000, transcendentals=0),
        name=name,
    )(*args)


def lay_out(xm, x2, b, body, rim):
    for c in range(2):
        lanes = slice(128 * c, 128 * c + 128)
        xm[b, 0:ROWS, lanes] = body[ROWS * c : ROWS * c + ROWS]
        xm[b, ROWS : ROWS + RIM, lanes] = rim[RIM * c : RIM * c + RIM]
    p, r = body[2 * ROWS :], rim[2 * RIM :]
    left = jnp.concatenate([p, swap(p), r, swap(r)], axis=0)
    right = jnp.concatenate([swap(p), p, swap(r), r], axis=0)
    n = ROWS + RIM
    x2[b, 0 : n - 16] = jnp.where(low_lanes(), left[0 : n - 16], right[16:n])
    x2[b, n - 16 : n] = jnp.where(low_lanes(), left[n - 16 : n], jnp.zeros((16, 128), left.dtype))


def lag_pair(ref, even, odd):
    pe, po = ref[even, 256:320], ref[odd, 256:320]
    rest = jnp.concatenate(
        [jnp.where(low_lanes(), pe, swap(po)), jnp.where(low_lanes(), swap(pe), po)], axis=0
    )
    return jnp.concatenate(
        [ref[even, 0:128], ref[even, 128:256], ref[odd, 0:128], ref[odd, 128:256], rest], axis=1
    )


def correlate_kernel(place_ref, keep_ref, got_ref, rimk_ref, rimg_ref, own_ref, oth_ref, out_ref, xm, x2, q):
    z, half = place_ref[0], place_ref[1]
    lay_out(xm, x2, 0, keep_ref, rimk_ref)
    lay_out(xm, x2, 1, got_ref, rimg_ref)

    te = jnp.zeros((2 * K * SUB, 128), jnp.float32)
    for s in range(2):
        ws = []
        for a in range(4 * s, 4 * s + 4):
            even = lax.rem(2 * a + 15 * z, 16)
            odd = lax.rem(2 * a + 1 + 15 * z, 16)
            w = jnp.concatenate([lag_pair(own_ref, 2 * a, 2 * a + 1), lag_pair(oth_ref, even, odd)], axis=0)
            wf = w.astype(jnp.float32)
            sq = wf * wf
            for j in range(5):
                te = te + sq[:, 128 * j : 128 * j + 128]
                ws.append(jnp.transpose(w[:, 128 * j : 128 * j + 128]))
        w = jnp.concatenate(ws, axis=0)
        for b in range(2):
            rows = []
            for a in range(4 * s, 4 * s + 4):
                r = 32 * a
                rows += [xm[b, r : r + USED], xm[b, r + 16 : r + 16 + USED], x2[b, r : r + USED]]
            part = lax.dot_general(jnp.concatenate(rows, axis=1), w, NN, preferred_element_type=jnp.float32)
            q[b, 0:USED, :] = part if s == 0 else q[b, 0:USED, :] + part
    te = jnp.sum(te.reshape(2, K, SUB, 128), axis=(0, 2))
    te = jnp.sum(te, axis=1, keepdims=True)

    lane = lax.broadcasted_iota(jnp.int32, (8, 128), 1)
    te_row = jnp.where(lane < 96, te[0:8], te[8:16])
    for b in range(2):
        q[b, USED:SPAN, :] = jnp.zeros((SPAN - USED, 2 * K * SUB), jnp.float32)
        sums = []
        for g in range(2):
            p = jnp.transpose(q[b, :, 128 * g : 128 * g + 128])
            p = p.reshape(K, SUB, SPAN)
            p = pltpu.roll(p, SPAN - (SUB - 1), 2, stride=1, stride_axis=1)
            sums.append(jnp.sum(p, axis=1))
        late = [pltpu.roll(p, SPAN - SUB, 1) for p in sums]
        stack = jnp.where(z == 1, late[0] + sums[1], sums[0] + late[1])

        sq = jnp.zeros((ROWS + RIM, 128), jnp.float32)
        for v in (xm[b, :, 0:128], xm[b, :, 128:256], jnp.where(low_lanes(), x2[b], jnp.zeros_like(x2[b]))):
            v = v.astype(jnp.float32)
            sq = sq + v * v
        de = jnp.sum(jnp.transpose(sq), axis=0, keepdims=True)
        de = jnp.broadcast_to(de, (8, ROWS + RIM))
        for i in range(8):
            de = de + pltpu.roll(de, ROWS + RIM - (1 << i), 1)

        at = 16 * jnp.where(half == b, 0, 1)
        for d in range(16):
            tile = slice(128 * (d // 2), 128 * (d // 2) + 128)
            lo, hi, en = stack[0:8, tile], stack[8:16, tile], de[:, tile]
            if d % 2 == 0:
                hi = pltpu.roll(hi, 64, 1)
            else:
                lo, en = pltpu.roll(lo, 64, 1), pltpu.roll(en, 64, 1)
            out_ref[at + d, 0:8, :] = jnp.where(lane < 64, lo, hi)
            out_ref[at + d, 8:16, :] = jnp.where(lane < 64, en, te_row)


def correlate(*args):
    return pl.pallas_call(
        correlate_kernel,
        out_shape=jax.ShapeDtypeStruct((32, 16, 128), jnp.float32),
        in_specs=[SMEM] + [VMEM] * 6,
        out_specs=VMEM,
        scratch_shapes=[
            pltpu.VMEM((2, ROWS + RIM, 256), jnp.bfloat16),
            pltpu.VMEM((2, ROWS + RIM, 128), jnp.bfloat16),
            pltpu.VMEM((2, SPAN, 2 * K * SUB), jnp.float32),
        ],
        compiler_params=pltpu.CompilerParams(vmem_limit_bytes=48 * 2**20),
        cost_estimate=pl.CostEstimate(flops=5_500_000_000, bytes_accessed=5_000_000, transcendentals=0),
        name="correlate",
    )(*args)


def finish_kernel(parts_ref, out_ref):
    total = jnp.sum(parts_ref[...], axis=0)
    scale = math.sqrt(L * CH)
    rows, energies = total[0:8], total[8:16]
    inv = lax.rsqrt(energies[:, 0:64] + 1e-06) * scale
    out_ref[0:8, :] = rows[:, 0:64] * inv * lax.rsqrt(energies[:, 64:65])
    out_ref[8:16, :] = rows[:, 64:128] * inv * lax.rsqrt(energies[:, 96:97])


def finish(parts):
    return pl.pallas_call(
        finish_kernel,
        out_shape=jax.ShapeDtypeStruct((K, 64), jnp.float32),
        in_specs=[VMEM],
        out_specs=VMEM,
        name="finish",
    )(parts)


def local(waveform, templates):
    tm = lax.axis_size("tm")
    chan = lax.axis_size("chan")
    me = lax.axis_index("tm")
    half = lax.rem(me // 8, 2)
    place = jnp.stack([lax.rem(me, 2), half, (me == tm - 1).astype(jnp.int32)])
    plane = [[2 * i + h for i in range(tm // 2)] for h in range(2)]
    partner = [(i, i ^ 8) for i in range(tm)]

    shard = jnp.flip(templates, 1).reshape(K * SUB, -1)
    ahead = jnp.concatenate([shard, waveform[:RIM]], axis=0)
    ahead = lax.ppermute(ahead, "tm", [(i, (i - 1) % tm) for i in range(tm)])

    keep, send, copies = packed(first_pack_kernel, ROWS, "first_pack", place, waveform, shard)
    got = lax.ppermute(send, "tm", partner)
    own = lax.all_to_all(copies, "tm", 0, 0, axis_index_groups=plane)

    rim_keep, rim_send, copies = packed(second_pack_kernel, RIM, "second_pack", place, ahead)
    rim_got = lax.ppermute(rim_send, "tm", partner)
    oth = lax.all_to_all(copies, "tm", 0, 0, axis_index_groups=plane)

    parts = correlate(place, keep, got, rim_keep, rim_got, own, oth)
    pairs = [
        [t * chan + c for t in (i, i ^ 8) for c in range(chan)] for i in range(tm) if i & 8 == 0
    ]
    parts = lax.all_to_all(parts, ("tm", "chan"), 0, 0, axis_index_groups=pairs)
    return finish(parts)


def solution(mesh):
    in_specs = (P("tm", "chan"), P(None, "tm", "chan"))
    out_specs = P(None, ("tm", "chan"))
    return jax.shard_map(local, mesh=mesh, in_specs=in_specs, out_specs=out_specs, check_vma=False)
```

time: 140 us -> 156 us (1.11)
  the two profiles are of different devices: /device:TPU:13 before, /device:TPU:1 now
where the time goes in v2:
time: 156 us; the launch traced here: 155 us
  waiting for transfers between devices  65.8 us (42%)
  starting transfers between devices  36.5 us (23%)
  blocking collectives  30.6 us (20%)
  Pallas kernels  12.7 us (8%)
  local copies, waits for them, and re-layouts  9.46 us (6%)
    ppermute x1, waiting for transfers between devices, local(): ahead = lax.ppermute(ahead, 'tm', [(i, (i - 1) % tm) for i in range(tm)])  39.1 us
    all_to_all x1, blocking collectives, local(): parts = lax.all_to_all(parts, ('tm', 'chan'), 0, 0, axis_index_groups=pairs)  30.6 us
    ppermute x1, waiting for transfers between devices, local(): rim_got = lax.ppermute(rim_send, 'tm', partner)  26.8 us
    ppermute x1, starting transfers between devices, local(): ahead = lax.ppermute(ahead, 'tm', [(i, (i - 1) % tm) for i in range(tm)])  19.8 us
    pallas_call x1, Pallas kernels, correlate(): pl.pallas_call(correlate_kernel, out_shape=jax.ShapeDtypeStruct((32, 16,...  7.94 us
    all_to_all x1, starting transfers between devices, local(): own = lax.all_to_all(copies, 'tm', 0, 0, axis_index_groups=plane)  7.72 us
    unnamed x14, local copies, waits for them, and re-layouts  7.1 us
    all_to_all x1, starting transfers between devices, local(): oth = lax.all_to_all(copies, 'tm', 0, 0, axis_index_groups=plane)  3.7 us
  transfers between devices with their start and end apart: 5, of which 2 were waited for; matrix products, arithmetic and copies ran while one was open for 0% of the time, Pallas kernels for 1%

profile of v2, /device:TPU:1, one launch (start us, length us, event | category | flops | bytes accessed | tf_op | source)
XLA Modules:
  0.0 155.4 jit_solution(577929221650783535)
XLA Ops:
  0.0 2.4 %rev.4 = bf16[16,8,640]{2,1,0:T(8,128)(2,1)S(1)} reverse(bf16[16,8,640]{2,1,0:T(8,128)(2,1)} %param.3), dimensions={1} | reverse | bytes 327680 | tf_op jit(solution)/shard_map/jit(_flip)/rev | solution.py:224
  2.4 0.1 pad_add_fusion.place_ref
  2.4 0.0 copy-start
  2.4 1.3 copy-done
  3.8 2.2 %first_pack.1 = (bf16[2560,128]{1,0:T(8,128)(2,1)S(1)}, bf16[2560,128]{1,0:T(8,128)(2,1)S(1)}, bf16[16,320,128]{2,1,0:T(8,128)(2,1)}) custom-call(s32[3]{0:T(128)S(1)} %pad_add_fusion.place_ref, bf16[1024,640]{1,0:T(8,128)(2,1)S(1)} %copy-done, bf16[128,640]{1,0:T(8,128)(2,1)S(1)} %bitcast.4), custom_call_target="tpu_custom_call" | custom-call | flops 2000000 | bytes 4000000 | tf_op jit(solution)/shard_map/first_pack/pallas_call | solution.py:83
  6.0 0.0 copy-start.2
  6.0 0.8 copy-done.2
  6.8 0.0 copy-start.4
  6.8 0.8 copy-done.4
  7.6 0.0 slice-start
  7.7 7.7 %all-to-all-start = ((bf16[16,320,128]{2,1,0:T(8,128)(2,1)}), bf16[16,320,128]{2,1,0:T(8,128)(2,1)S(1)}, u32[]{:S(2)}, u32[]{:S(2)}) async-start(bf16[16,320,128]{2,1,0:T(8,128)(2,1)} %get-tuple-element.15), calls=%async_computation | async-start | bytes 2621440 | tf_op jit(solution)/shard_map/all_to_all | solution.py:230
  15.4 0.0 slice-done
  15.4 19.8 %collective-permute-start.1 = (bf16[384,640]{1,0:T(8,128)(2,1)S(1)}, bf16[384,640]{1,0:T(8,128)(2,1)S(1)}, u32[]{:S(2)}, u32[]{:S(2)}) collective-permute-start(bf16[384,640]{1,0:T(8,128)(2,1)S(1)} %pad_maximum_fusion), channel_id=1, source_target_pairs={{0,496},{16,0},{32,16},{48,32},{64,48},{80,64},{96,80},{112,96},{1... | collective-permute-start | bytes 1474568 | tf_op jit(solution)/shard_map/ppermute | solution.py:226
  35.3 39.1 %collective-permute-done.1.c_ref = bf16[384,640]{1,0:T(8,128)(2,1)S(1)} collective-permute-done((bf16[384,640]{1,0:T(8,128)(2,1)S(1)}, bf16[384,640]{1,0:T(8,128)(2,1)S(1)}, u32[]{:S(2)}, u32[]{:S(2)}) %collective-permute-start.1) | collective-permute-done | bytes 491552 | tf_op jit(solution)/shard_map/ppermute | solution.py:226
  74.4 0.8 second_pack.1
  75.2 0.0 copy-start.1
  75.2 1.1 copy-done.1
  76.3 0.0 all-to-all-done.own_ref
  76.3 3.7 %all-to-all-start.1 = ((bf16[16,320,128]{2,1,0:T(8,128)(2,1)}), bf16[16,320,128]{2,1,0:T(8,128)(2,1)S(1)}, u32[]{:S(2)}, u32[]{:S(2)}) async-start(bf16[16,320,128]{2,1,0:T(8,128)(2,1)} %copy-done.1), calls=%async_computation.1 | async-start | bytes 2621440 | tf_op jit(solution)/shard_map/all_to_all | solution.py:234
  80.0 3.2 %collective-permute-start = (bf16[2560,128]{1,0:T(8,128)(2,1)}, bf16[2560,128]{1,0:T(8,128)(2,1)S(1)}, u32[]{:S(2)}, u32[]{:S(2)}) collective-permute-start(bf16[2560,128]{1,0:T(8,128)(2,1)} %copy-done.4), channel_id=1, source_target_pairs={{0,128},{16,144},{32,160},{48,176},{64,192},{80,208},{96,224},{112... | collective-permute-start | bytes 1966088 | tf_op jit(solution)/shard_map/ppermute | solution.py:229
  83.1 2.1 %collective-permute-start.2 = (bf16[640,128]{1,0:T(8,128)(2,1)S(1)}, bf16[640,128]{1,0:T(8,128)(2,1)S(1)}, u32[]{:S(2)}, u32[]{:S(2)}) collective-permute-start(bf16[640,128]{1,0:T(8,128)(2,1)S(1)} %get-tuple-element.14), channel_id=1, source_target_pairs={{0,128},{16,144},{32,160},{48,176},{64,192},{80,208},{96,224},{112... | collective-permute-start | bytes 491528 | tf_op jit(solution)/shard_map/ppermute | solution.py:233
  85.3 26.8 %collective-permute-done.2.rimg_ref = bf16[640,128]{1,0:T(8,128)(2,1)S(1)} collective-permute-done((bf16[640,128]{1,0:T(8,128)(2,1)S(1)}, bf16[640,128]{1,0:T(8,128)(2,1)S(1)}, u32[]{:S(2)}, u32[]{:S(2)}) %collective-permute-start.2) | collective-permute-done | bytes 163872 | tf_op jit(solution)/shard_map/ppermute | solution.py:233
  112.0 0.0 collective-permute-done.got_ref
  112.0 0.0 copy-start.5
  112.0 0.8 copy-done.5
  112.9 0.0 all-to-all-done.1.oth_ref
  112.9 0.0 copy-start.3
  112.9 1.1 copy-done.3
  114.0 0.0 copy-start.6
  114.0 1.1 copy-done.6
  115.1 7.9 %correlate.1 = f32[32,16,128]{2,1,0:T(8,128)S(1)} custom-call(s32[3]{0:T(128)S(1)} %pad_add_fusion.place_ref, bf16[2560,128]{1,0:T(8,128)(2,1)S(1)} %copy-done.3, bf16[2560,128]{1,0:T(8,128)(2,1)S(1)} %copy-done.6, bf16[640,128]{1,0:T(8,128)(2,1)S(1)} %get-tuple-element.13.rimk_ref, bf16[640,128]{1,0:T(8,128)(2,1)S(1)} %collective-permute-done.2.rimg_ref, ...), custom_call_target="tpu_custom_call" | custom-call | flops 5500000256 | bytes 5000000 | tf_op jit(solution)/shard_map/correlate/pallas_call | solution.py:180
  123.0 30.6 %all_to_all.15.parts_ref = f32[32,16,128]{2,1,0:T(8,128)} all-to-all(f32[32,16,128]{2,1,0:T(8,128)S(1)} %correlate.1), channel_id=1, replica_groups={{0,1,2,3,4,5,6,7,8,9,10,11,12,13,14,15,128,129,130,131,132,133,134,135,..., dimensions={0} | all-to-all | bytes 524288 | tf_op jit(solution)/shard_map/all_to_all | solution.py:240
  153.6 1.7 %finish.1 = f32[16,64]{1,0:T(8,128)} custom-call(f32[32,16,128]{2,1,0:T(8,128)} %all_to_all.15.parts_ref), custom_call_target="tpu_custom_call" | custom-call | tf_op jit(solution)/shard_map/finish/pallas_call | solution.py:206
  (1 shorter events, 0.0 us)
Async XLA Ops:
  2.4 1.3 copy-start
  6.0 0.9 copy-start.2
  6.8 0.8 copy-start.4
  7.6 7.7 %slice-start = ((bf16[1024,640]{1,0:T(8,128)(2,1)}), bf16[256,640]{1,0:T(8,128)(2,1)S(1)}, s32[]{:S(2)}) async-start(bf16[1024,640]{1,0:T(8,128)(2,1)} %x_ref.1), calls=%async_computation.3 | async-start | bytes 655360 | tf_op jit(solution)/shard_map/slice | solution.py:225
  7.7 68.6 %all-to-all-start = ((bf16[16,320,128]{2,1,0:T(8,128)(2,1)}), bf16[16,320,128]{2,1,0:T(8,128)(2,1)S(1)}, u32[]{:S(2)}, u32[]{:S(2)}) async-start(bf16[16,320,128]{2,1,0:T(8,128)(2,1)} %get-tuple-element.15), calls=%async_computation | async-start | bytes 2621440 | tf_op jit(solution)/shard_map/all_to_all | solution.py:230
  15.4 58.9 %collective-permute-start.1 = (bf16[384,640]{1,0:T(8,128)(2,1)S(1)}, bf16[384,640]{1,0:T(8,128)(2,1)S(1)}, u32[]{:S(2)}, u32[]{:S(2)}) collective-permute-start(bf16[384,640]{1,0:T(8,128)(2,1)S(1)} %pad_maximum_fusion), channel_id=1, source_target_pairs={{0,496},{16,0},{32,16},{48,32},{64,48},{80,64},{96,80},{112,96},{1... | collective-permute-start | bytes 1474568 | tf_op jit(solution)/shard_map/ppermute | solution.py:226
  75.2 1.1 copy-start.1
  76.3 36.6 %all-to-all-start.1 = ((bf16[16,320,128]{2,1,0:T(8,128)(2,1)}), bf16[16,320,128]{2,1,0:T(8,128)(2,1)S(1)}, u32[]{:S(2)}, u32[]{:S(2)}) async-start(bf16[16,320,128]{2,1,0:T(8,128)(2,1)} %copy-done.1), calls=%async_computation.1 | async-start | bytes 2621440 | tf_op jit(solution)/shard_map/all_to_all | solution.py:234
  80.0 32.1 %collective-permute-start = (bf16[2560,128]{1,0:T(8,128)(2,1)}, bf16[2560,128]{1,0:T(8,128)(2,1)S(1)}, u32[]{:S(2)}, u32[]{:S(2)}) collective-permute-start(bf16[2560,128]{1,0:T(8,128)(2,1)} %copy-done.4), channel_id=1, source_target_pairs={{0,128},{16,144},{32,160},{48,176},{64,192},{80,208},{96,224},{112... | collective-permute-start | bytes 1966088 | tf_op jit(solution)/shard_map/ppermute | solution.py:229
  83.1 28.9 %collective-permute-start.2 = (bf16[640,128]{1,0:T(8,128)(2,1)S(1)}, bf16[640,128]{1,0:T(8,128)(2,1)S(1)}, u32[]{:S(2)}, u32[]{:S(2)}) collective-permute-start(bf16[640,128]{1,0:T(8,128)(2,1)S(1)} %get-tuple-element.14), channel_id=1, source_target_pairs={{0,128},{16,144},{32,160},{48,176},{64,192},{80,208},{96,224},{112... | collective-permute-start | bytes 491528 | tf_op jit(solution)/shard_map/ppermute | solution.py:233
  112.0 0.8 copy-start.5
  112.9 1.1 copy-start.3
  114.0 1.1 copy-start.6

commit v3 on v1

v3 whole, which is shorter than its diff:
```python
import math

import jax
import jax.numpy as jnp
from jax import lax
from jax.experimental import pallas as pl
from jax.experimental.pallas import tpu as pltpu
from jax.sharding import PartitionSpec as P

CH = 10240
L = 256
K = 16
SUB = 8
ROWS = 1024
RIM = 256
USED = ROWS + 16
SPAN = ROWS + 128
EDGE_USED = RIM + 16
EDGE_SPAN = RIM + 128
NN = (((1,), (0,)), ((), ()))
BF16 = jnp.bfloat16
VMEM = pl.BlockSpec(memory_space=pltpu.VMEM)
SMEM = pl.BlockSpec(memory_space=pltpu.SMEM)
ANY = pl.BlockSpec(memory_space=pl.ANY)


def swap(v):
    return jnp.concatenate([v[:, 64:], v[:, :64]], axis=1)


def low_lanes():
    return lax.broadcasted_iota(jnp.int32, (1, 128), 1) < 64


def pack_rest(v, half):
    n = v.shape[0] // 2
    if half == 0:
        return jnp.where(low_lanes(), v[:n], swap(v[n:]))
    return jnp.where(low_lanes(), swap(v[:n]), v[n:])


def pack_half(v, half, upper):
    return [
        jnp.where(upper, v[:, 256:384], v[:, 0:128]),
        jnp.where(upper, v[:, 384:512], v[:, 128:256]),
        jnp.where(upper, pack_rest(v[:, 512:640], 1), pack_rest(v[:, 512:640], 0)),
    ]


def first_pack_kernel(place, x, send):
    at = 0
    for part in pack_half(x[...], None, place[1] == 0):
        send[at : at + part.shape[0]] = part
        at += part.shape[0]


def lag_pack_kernel(lags, copies, packed, sems):
    i = lax.broadcasted_iota(jnp.int32, (K * SUB, K * SUB), 0)
    j = lax.broadcasted_iota(jnp.int32, (K * SUB, K * SUB), 1)
    order = (i // SUB * SUB + (SUB - 1 - i % SUB) == j).astype(BF16)
    v = lax.dot_general(order, lags[...], NN, preferred_element_type=jnp.float32).astype(BF16)
    for half in range(2):
        packed[half, 0:128] = v[:, 256 * half : 256 * half + 128]
        packed[half, 128:256] = v[:, 256 * half + 128 : 256 * half + 256]
        packed[half, 256:320] = pack_rest(v[:, 512:640], half)
    moves = [pltpu.make_async_copy(packed.at[p // 8], copies.at[p], sems.at[p]) for p in range(16)]
    for move in moves:
        move.start()
    for move in moves:
        move.wait()


def first_pack(place, x):
    return pl.pallas_call(
        first_pack_kernel,
        out_shape=jax.ShapeDtypeStruct((ROWS * 5 // 2, 128), BF16),
        in_specs=[SMEM, VMEM],
        out_specs=VMEM,
        compiler_params=pltpu.CompilerParams(vmem_limit_bytes=16 * 2**20),
        cost_estimate=pl.CostEstimate(flops=2_000_000, bytes_accessed=2_000_000, transcendentals=0),
        name="first_pack",
    )(place, x)


def lag_pack(lags):
    return pl.pallas_call(
        lag_pack_kernel,
        out_shape=jax.ShapeDtypeStruct((16, 320, 128), BF16),
        in_specs=[VMEM],
        out_specs=ANY,
        scratch_shapes=[pltpu.VMEM((2, 320, 128), BF16), pltpu.SemaphoreType.DMA((16,))],
        cost_estimate=pl.CostEstimate(flops=2_000_000, bytes_accessed=1_500_000, transcendentals=0),
        name="lag_pack",
    )(lags)


def lanes_of(half, c):
    return pl.ds(pl.multiple_of(256 * half + 128 * c, 128), 128)


def lag_pair(ref, even, odd):
    pe, po = ref[even, 256:320], ref[odd, 256:320]
    rest = jnp.concatenate(
        [jnp.where(low_lanes(), pe, swap(po)), jnp.where(low_lanes(), swap(pe), po)], axis=0
    )
    return jnp.concatenate(
        [ref[even, 0:128], ref[even, 128:256], ref[odd, 0:128], ref[odd, 128:256], rest], axis=1
    )


def sum_lags(xm, x2, q, own, oth, used, with_energy):
    te = jnp.zeros((2 * K * SUB, 128), jnp.float32)
    for s in range(2):
        ws = []
        for a in range(4 * s, 4 * s + 4):
            w = jnp.concatenate([lag_pair(ref, 2 * a, 2 * a + 1) for ref in (own, oth)], axis=0)
            if with_energy:
                wf = w.astype(jnp.float32)
                sq = wf * wf
                for j in range(5):
                    te = te + sq[:, 128 * j : 128 * j + 128]
            for j in range(5):
                ws.append(jnp.transpose(w[:, 128 * j : 128 * j + 128]))
        w = jnp.concatenate(ws, axis=0)
        for b in range(2):
            rows = []
            for a in range(4 * s, 4 * s + 4):
                r = 32 * a
                rows += [xm[b, r : r + used], xm[b, r + 16 : r + 16 + used], x2[b, r : r + used]]
            part = lax.dot_general(jnp.concatenate(rows, axis=1), w, NN, preferred_element_type=jnp.float32)
            q[b, 0:used, :] = part if s == 0 else q[b, 0:used, :] + part
    te = jnp.sum(te.reshape(2, K, SUB, 128), axis=(0, 2))
    te = jnp.sum(te, axis=1, keepdims=True)
    lane = lax.broadcasted_iota(jnp.int32, (K, 128), 1)
    row = lax.broadcasted_iota(jnp.int32, (K, 128), 0)
    return jnp.sum(jnp.where(lane == 64 + row, te, 0.0), axis=0, keepdims=True)


def sum_fine_lags(q, b, span, used, z):
    q[b, used:span, :] = jnp.zeros((span - used, 2 * K * SUB), jnp.float32)
    sums = []
    for g in range(2):
        p = jnp.transpose(q[b, :, 128 * g : 128 * g + 128])
        p = p.reshape(K, SUB, span)
        p = pltpu.roll(p, span - (SUB - 1), 2, stride=1, stride_axis=1)
        sums.append(jnp.sum(p, axis=1))
    late = [pltpu.roll(p, span - SUB, 1) for p in sums]
    return jnp.where(z == 1, late[0] + sums[1], sums[0] + late[1])


def window_energy(xm, x2, b, n):
    sq = jnp.zeros((n, 128), jnp.float32)
    rest = x2[b, 0:n]
    for v in (xm[b, 0:n, 0:128], xm[b, 0:n, 128:256], jnp.where(low_lanes(), rest, jnp.zeros_like(rest))):
        v = v.astype(jnp.float32)
        sq = sq + v * v
    de = jnp.sum(jnp.transpose(sq), axis=0, keepdims=True)
    de = jnp.broadcast_to(de, (8, n))
    for i in range(8):
        de = de + pltpu.roll(de, n - (1 << i), 1)
    return de


def store(out, at, stack, de, te_row, count):
    low = low_lanes()
    for d in range(count):
        tile = slice(128 * (d // 2), 128 * (d // 2) + 128)
        lo, hi, en = stack[0:8, tile], stack[8:16, tile], de[:, tile]
        if d % 2 == 0:
            hi = pltpu.roll(hi, 64, 1)
        else:
            lo, en = pltpu.roll(lo, 64, 1), pltpu.roll(en, 64, 1)
        both = jnp.where(low, lo, hi)
        for r in range(8):
            out[at + d, :, 128 * r : 128 * r + 128] = both[r : r + 1]
        out[at + d, :, 1024:1152] = jnp.where(low, en[0:1], te_row)


def lay_out_rest(x2, b, left, right, before, after):
    zeros = [jnp.zeros((n, 128), BF16) for n in (before, after)]
    left = jnp.concatenate([v for v in (zeros[0], left, zeros[1]) if v.shape[0]], axis=0)
    right = jnp.concatenate([v for v in (zeros[0], right, zeros[1]) if v.shape[0]], axis=0)
    n = left.shape[0]
    x2[b, 0 : n - 16] = jnp.where(low_lanes(), left[0 : n - 16], right[16:n])
    x2[b, n - 16 : n] = jnp.where(low_lanes(), left[n - 16 : n], jnp.zeros((16, 128), BF16))


def fetch(x, got, own, oth, half, rows, at, xm, mine, his, lo_lags, hi_lags, sems):
    first = [
        pltpu.make_async_copy(x.at[pl.ds(0, rows), pl.ds(512, 128)], mine, sems.at[0]),
        pltpu.make_async_copy(got.at[pl.ds(2 * ROWS, his.shape[0])], his, sems.at[1]),
    ]
    second = [
        pltpu.make_async_copy(own, lo_lags, sems.at[2]),
        pltpu.make_async_copy(oth, hi_lags, sems.at[3]),
    ]
    for c in range(2):
        lanes, body = pl.ds(128 * c, 128), pl.ds(at, rows)
        second += [
            pltpu.make_async_copy(x.at[pl.ds(0, rows), lanes_of(half, c)], xm.at[0, body, lanes], sems.at[4 + c]),
            pltpu.make_async_copy(got.at[pl.ds(ROWS * c, rows)], xm.at[1, body, lanes], sems.at[6 + c]),
        ]
    for move in first + second:
        move.start()
    return first, second


def edge_kernel(place, x, got, own, oth, edges, xm, x2, q, mine, his, lo_lags, hi_lags, sums, sems):
    z, half = place[0], place[1]
    first, second = fetch(x, got, own, oth, half, RIM, RIM, xm, mine, his, lo_lags, hi_lags, sems)
    for move in first:
        move.wait()
    for b in range(2):
        xm[b, 0:RIM] = jnp.zeros((RIM, 256), BF16)
        if b == 0:
            v = mine[...]
            left, right = jnp.where(half == 1, swap(v), v), jnp.where(half == 1, v, swap(v))
        else:
            p = his[...]
            left, right = p, swap(p)
        lay_out_rest(x2, b, left, right, RIM, 0)
    for move in second:
        move.wait()
    sum_lags(xm, x2, q, lo_lags, hi_lags, EDGE_USED, False)
    for b in range(2):
        stack = sum_fine_lags(q, b, EDGE_SPAN, EDGE_USED, z)
        de = window_energy(xm, x2, b, 2 * RIM)
        store(sums, 4 * b, stack, de, jnp.zeros((1, 128), jnp.float32), 4)
    low = jnp.where(half == 1, sums[4:8], sums[0:4])
    high = jnp.where(half == 1, sums[0:4], sums[4:8])
    turn = place[2] == 1
    edges[0:4] = jnp.where(turn, high, low)
    edges[4:8] = jnp.where(turn, jnp.zeros_like(high), high)


def main_kernel(place, x, got, own, oth, out, xm, x2, q, mine, his, lo_lags, hi_lags, sems):
    z, half = place[0], place[1]
    first, second = fetch(x, got, own, oth, half, ROWS, 0, xm, mine, his, lo_lags, hi_lags, sems)
    for move in first:
        move.wait()
    for b in range(2):
        xm[b, ROWS:] = jnp.zeros((RIM, 256), BF16)
        if b == 0:
            v = mine[...]
            left, right = jnp.where(half == 1, swap(v), v), jnp.where(half == 1, v, swap(v))
        else:
            p = his[...]
            left, right = jnp.concatenate([p, swap(p)], axis=0), jnp.concatenate([swap(p), p], axis=0)
        lay_out_rest(x2, b, left, right, 0, RIM)
    for move in second:
        move.wait()
    te_row = sum_lags(xm, x2, q, lo_lags, hi_lags, USED, True)
    for b in range(2):
        stack = sum_fine_lags(q, b, SPAN, USED, z)
        de = window_energy(xm, x2, b, ROWS + RIM)
        store(out, 16 * jnp.where(half == b, 0, 1), stack, de, te_row, 16)


def scratch(rows, span, his_rows):
    return [
        pltpu.VMEM((2, rows + RIM, 256), BF16),
        pltpu.VMEM((2, rows + RIM, 128), BF16),
        pltpu.VMEM((2, span, 2 * K * SUB), jnp.float32),
        pltpu.VMEM((rows, 128), BF16),
        pltpu.VMEM((his_rows, 128), BF16),
        pltpu.VMEM((16, 320, 128), BF16),
        pltpu.VMEM((16, 320, 128), BF16),
    ]


def edge_sums(*args):
    return pl.pallas_call(
        edge_kernel,
        out_shape=jax.ShapeDtypeStruct((8, 1, 1152), jnp.float32),
        in_specs=[SMEM] + [ANY] * 4,
        out_specs=VMEM,
        scratch_shapes=scratch(RIM, EDGE_SPAN, RIM)
        + [pltpu.VMEM((8, 1, 1152), jnp.float32), pltpu.SemaphoreType.DMA((8,))],
        compiler_params=pltpu.CompilerParams(vmem_limit_bytes=32 * 2**20),
        cost_estimate=pl.CostEstimate(flops=1_400_000_000, bytes_accessed=3_200_000, transcendentals=0),
        name="edge_sums",
    )(*args)


def main_sums(*args):
    return pl.pallas_call(
        main_kernel,
        out_shape=jax.ShapeDtypeStruct((32, 1, 1152), jnp.float32),
        in_specs=[SMEM] + [ANY] * 4,
        out_specs=VMEM,
        scratch_shapes=scratch(ROWS, SPAN, ROWS // 2) + [pltpu.SemaphoreType.DMA((8,))],
        compiler_params=pltpu.CompilerParams(vmem_limit_bytes=48 * 2**20),
        cost_estimate=pl.CostEstimate(flops=5_500_000_000, bytes_accessed=5_000_000, transcendentals=0),
        name="main_sums",
    )(*args)


def finish_kernel(parts, out):
    total = jnp.sum(parts[...], axis=0)
    scale = math.sqrt(L * CH)
    rows = jnp.concatenate([total[:, 128 * r : 128 * r + 128] for r in range(8)], axis=0)
    last = total[:, 1024:1152]
    lane = lax.broadcasted_iota(jnp.int32, (K, 128), 1)
    row = lax.broadcasted_iota(jnp.int32, (K, 128), 0)
    te = jnp.sum(jnp.where(lane == 64 + row, last, 0.0), axis=1, keepdims=True)
    both = jnp.concatenate([rows[:, 0:64], rows[:, 64:128]], axis=0)
    out[...] = both * scale * lax.rsqrt(last[:, 0:64] + 1e-06) * lax.rsqrt(te)


def finish(parts):
    return pl.pallas_call(
        finish_kernel,
        out_shape=jax.ShapeDtypeStruct((K, 64), jnp.float32),
        in_specs=[VMEM],
        out_specs=VMEM,
        name="finish",
    )(parts)


def local(waveform, templates):
    tm = lax.axis_size("tm")
    chan = lax.axis_size("chan")
    me = lax.axis_index("tm")
    half = me // 16
    turn = jnp.logical_and(lax.rem(me, 8) == 0, lax.rem(me // 8, 2) == 0)
    place = jnp.stack([lax.rem(me, 2), half, turn.astype(jnp.int32)])
    plane = [[2 * i + h for i in range(tm // 2)] for h in range(2)]
    partner = [(i, i ^ 16) for i in range(tm)]

    shard = templates.reshape(K * SUB, -1)
    other = lax.ppermute(shard, "tm", [(i, i ^ 1) for i in range(tm)])
    got = lax.ppermute(first_pack(place, waveform), "tm", partner)

    def spread(lags):
        return lax.all_to_all(lag_pack(lags), "tm", 0, 0, axis_index_groups=plane)

    own = spread(shard)
    other, got = lax.optimization_barrier((other, got))
    oth = spread(other)

    edges = edge_sums(place, waveform, got, own, oth)
    edges = lax.ppermute(edges, "tm", [(i, i - 1 if i % 8 else (i ^ 8) + 7) for i in range(tm)])

    parts = main_sums(place, waveform, got, own, oth)
    edges = jnp.pad(edges.reshape(2, 4, 1, 1152), ((0, 0), (12, 0), (0, 0), (0, 0)))
    parts = parts + edges.reshape(parts.shape)
    pairs = [[t * chan + c for t in (i, i ^ 16) for c in range(chan)] for i in range(tm // 2)]
    parts = lax.all_to_all(parts, ("tm", "chan"), 0, 0, axis_index_groups=pairs)
    return finish(parts)


def solution(mesh):
    in_specs = (P("tm", "chan"), P(None, "tm", "chan"))
    out_specs = P(None, ("tm", "chan"))
    return jax.shard_map(local, mesh=mesh, in_specs=in_specs, out_specs=out_specs, check_vma=False)
```

time: 140 us -> 123 us (0.88)
  the two profiles are of different devices: /device:TPU:13 before, /device:TPU:1 now
where the time goes in v3:
time: 123 us; the launch traced here: 122 us
  starting transfers between devices  47.6 us (39%)
  blocking collectives  46.4 us (38%)
  Pallas kernels  19.9 us (16%)
  waiting for transfers between devices  7.27 us (6%)
    all_to_all x1, blocking collectives, local(): parts = lax.all_to_all(parts, ('tm', 'chan'), 0, 0, axis_index_groups=pairs)  26.5 us
    all_to_all x1, blocking collectives, spread(): return lax.all_to_all(lag_pack(lags), 'tm', 0, 0, axis_index_groups=plane)  19.9 us
    ppermute x1, starting transfers between devices, local(): lax.ppermute(edges, 'tm', [(i, i - 1 if i % 8 else (i ^ 8) + 7) for i in...  19.6 us
    ppermute x1, starting transfers between devices, local(): other = lax.ppermute(shard, 'tm', [(i, i ^ 1) for i in range(tm)])  15.4 us
    pallas_call x1, Pallas kernels, main_sums(): pl.pallas_call(main_kernel, out_shape=jax.ShapeDtypeStruct((32, 1, 1152),...  8.78 us
    all_to_all x1, starting transfers between devices, spread(): return lax.all_to_all(lag_pack(lags), 'tm', 0, 0, axis_index_groups=plane)  7.72 us
    pallas_call x2, Pallas kernels, lag_pack(): pl.pallas_call(lag_pack_kernel, out_shape=jax.ShapeDtypeStruct((16, 320,...  4.78 us
    ppermute x1, starting transfers between devices, local(): got = lax.ppermute(first_pack(place, waveform), 'tm', partner)  4.78 us
  transfers between devices with their start and end apart: 4, of which 2 were waited for; matrix products, arithmetic and copies ran while one was open for 0% of the time, Pallas kernels for 10%

profile of v3, /device:TPU:1, one launch (start us, length us, event | category | flops | bytes accessed | tf_op | source)
XLA Modules:
  0.0 122.4 jit_solution(13459034096050086569)
XLA Ops:
  0.0 2.4 %lag_pack.2 = bf16[16,320,128]{2,1,0:T(8,128)(2,1)} custom-call(bf16[128,640]{1,0:T(8,128)(2,1)} %bitcast.7), custom_call_target="tpu_custom_call" | custom-call | flops 2000000 | bytes 1500000 | tf_op jit(solution)/shard_map/lag_pack/pallas_call | solution.py:86
  2.4 0.0 copy-start
  2.4 7.7 %all-to-all-start = ((bf16[16,320,128]{2,1,0:T(8,128)(2,1)}), bf16[16,320,128]{2,1,0:T(8,128)(2,1)S(1)}, u32[]{:S(2)}, u32[]{:S(2)}) async-start(bf16[16,320,128]{2,1,0:T(8,128)(2,1)} %lag_pack.2), calls=%async_computation | async-start | bytes 2621440 | tf_op jit(solution)/shard_map/all_to_all | solution.py:335
  10.1 0.0 copy-start.1
  10.2 0.1 pad_add_fusion.place
  10.3 0.0 copy-done
  10.3 0.8 first_pack.1
  11.1 4.8 %collective-permute-start.1 = (bf16[2560,128]{1,0:T(8,128)(2,1)S(1)}, bf16[2560,128]{1,0:T(8,128)(2,1)S(1)}, u32[]{:S(2)}, u32[]{:S(2)}) collective-permute-start(bf16[2560,128]{1,0:T(8,128)(2,1)S(1)} %first_pack.1), channel_id=1, source_target_pairs={{0,256},{16,272},{32,288},{48,304},{64,320},{80,336},{96,352},{112... | collective-permute-start | bytes 1966088 | tf_op jit(solution)/shard_map/ppermute | solution.py:332
  15.8 0.0 copy-done.1
  15.9 15.4 %collective-permute-start = (bf16[128,640]{1,0:T(8,128)(2,1)S(1)}, bf16[128,640]{1,0:T(8,128)(2,1)S(1)}, u32[]{:S(2)}, u32[]{:S(2)}) collective-permute-start(bf16[128,640]{1,0:T(8,128)(2,1)S(1)} %bitcast.8), channel_id=1, source_target_pairs={{0,16},{16,0},{32,48},{48,32},{64,80},{80,64},{96,112},{112,96},{1... | collective-permute-start | bytes 491528 | tf_op jit(solution)/shard_map/ppermute | solution.py:331
  31.3 3.0 %collective-permute-done.lags = bf16[128,640]{1,0:T(8,128)(2,1)S(1)} collective-permute-done((bf16[128,640]{1,0:T(8,128)(2,1)S(1)}, bf16[128,640]{1,0:T(8,128)(2,1)S(1)}, u32[]{:S(2)}, u32[]{:S(2)}) %collective-permute-start) | collective-permute-done | bytes 163872 | tf_op jit(solution)/shard_map/ppermute | solution.py:331
  34.3 0.0 copy-start.2
  34.3 0.7 copy-done.2
  35.0 4.3 %collective-permute-done.1.got = bf16[2560,128]{1,0:T(8,128)(2,1)S(1)} collective-permute-done((bf16[2560,128]{1,0:T(8,128)(2,1)S(1)}, bf16[2560,128]{1,0:T(8,128)(2,1)S(1)}, u32[]{:S(2)}, u32[]{:S(2)}) %collective-permute-start.1) | collective-permute-done | bytes 655392 | tf_op jit(solution)/shard_map/ppermute | solution.py:332
  39.2 2.4 %lag_pack.3 = bf16[16,320,128]{2,1,0:T(8,128)(2,1)} custom-call(bf16[128,640]{1,0:T(8,128)(2,1)} %copy-done.2), custom_call_target="tpu_custom_call" | custom-call | flops 2000000 | bytes 1500000 | tf_op jit(solution)/shard_map/lag_pack/pallas_call | solution.py:86
  41.6 0.0 all-to-all-done.own
  41.7 19.9 %all_to_all.15.oth = bf16[16,320,128]{2,1,0:T(8,128)(2,1)S(1)} all-to-all(bf16[16,320,128]{2,1,0:T(8,128)(2,1)} %lag_pack.3), channel_id=1, replica_groups={{0,32,64,96,128,160,192,224,256,288,320,352,384,416,448,480},{16,48,80,..., dimensions={0} | all-to-all | bytes 2621440 | tf_op jit(solution)/shard_map/all_to_all | solution.py:335
  61.6 3.9 %edge_sums.1 = f32[8,1,1152]{2,1,0:T(1,128)S(1)} custom-call(s32[3]{0:T(128)S(1)} %pad_add_fusion.place, bf16[1024,640]{1,0:T(8,128)(2,1)S(1)} %copy-done, bf16[2560,128]{1,0:T(8,128)(2,1)S(1)} %collective-permute-done.1.got, bf16[16,320,128]{2,1,0:T(8,128)(2,1)S(1)} %all-to-all-done.own, bf16[16,320,128]{2,1,0:T(8,128)(2,1)S(1)} %all_to_all.15.oth), custom_call_target="tpu_custom_call" | custom-call | flops 1400000000 | bytes 3200000 | tf_op jit(solution)/shard_map/edge_sums/pallas_call | solution.py:272
  65.5 19.6 %collective-permute-start.2 = (f32[8,1,1152]{2,1,0:T(1,128)S(1)}, f32[8,1,1152]{2,1,0:T(1,128)S(1)}, u32[]{:S(2)}, u32[]{:S(2)}) collective-permute-start(f32[8,1,1152]{2,1,0:T(1,128)S(1)} %edge_sums.1), channel_id=1, source_target_pairs={{0,240},{16,0},{32,16},{48,32},{64,48},{80,64},{96,80},{112,96},{1... | collective-permute-start | bytes 110600 | tf_op jit(solution)/shard_map/ppermute | solution.py:342
  85.1 8.8 %main_sums.1 = f32[32,1,1152]{2,1,0:T(1,128)S(1)} custom-call(s32[3]{0:T(128)S(1)} %pad_add_fusion.place, bf16[1024,640]{1,0:T(8,128)(2,1)S(1)} %copy-done, bf16[2560,128]{1,0:T(8,128)(2,1)S(1)} %collective-permute-done.1.got, bf16[16,320,128]{2,1,0:T(8,128)(2,1)S(1)} %all-to-all-done.own, bf16[16,320,128]{2,1,0:T(8,128)(2,1)S(1)} %all_to_all.15.oth), custom_call_target="tpu_custom_call" | custom-call | flops 5500000256 | bytes 5000000 | tf_op jit(solution)/shard_map/main_sums/pallas_call | solution.py:286
  93.9 0.0 collective-permute-done.2
  93.9 0.1 pad.4
  94.0 0.2 bitcast_add_fusion
  94.2 26.5 %all_to_all.16.parts = f32[32,1,1152]{2,1,0:T(1,128)} all-to-all(f32[32,1,1152]{2,1,0:T(1,128)S(1)} %bitcast_add_fusion), channel_id=1, replica_groups={{0,1,2,3,4,5,6,7,8,9,10,11,12,13,14,15,256,257,258,259,260,261,262,263,..., dimensions={0} | all-to-all | bytes 294912 | tf_op jit(solution)/shard_map/all_to_all | solution.py:348
  120.7 1.7 %finish.1 = f32[16,64]{1,0:T(8,128)} custom-call(f32[32,1,1152]{2,1,0:T(1,128)} %all_to_all.16.parts), custom_call_target="tpu_custom_call" | custom-call | tf_op jit(solution)/shard_map/finish/pallas_call | solution.py:311
Async XLA Ops:
  2.4 7.9 %copy-start = (bf16[1024,640]{1,0:T(8,128)(2,1)S(1)}, bf16[1024,640]{1,0:T(8,128)(2,1)}, u32[]{:S(2)}) copy-start(bf16[1024,640]{1,0:T(8,128)(2,1)} %x.7) | copy-start | bytes 3932164
  2.4 39.2 %all-to-all-start = ((bf16[16,320,128]{2,1,0:T(8,128)(2,1)}), bf16[16,320,128]{2,1,0:T(8,128)(2,1)S(1)}, u32[]{:S(2)}, u32[]{:S(2)}) async-start(bf16[16,320,128]{2,1,0:T(8,128)(2,1)} %lag_pack.2), calls=%async_computation | async-start | bytes 2621440 | tf_op jit(solution)/shard_map/all_to_all | solution.py:335
  10.1 5.7 %copy-start.1 = (bf16[16,8,640]{2,1,0:T(8,128)(2,1)S(1)}, bf16[16,8,640]{2,1,0:T(8,128)(2,1)}, u32[]{:S(2)}) copy-start(bf16[16,8,640]{2,1,0:T(8,128)(2,1)} %param.3) | copy-start | bytes 491524
  11.1 28.2 %collective-permute-start.1 = (bf16[2560,128]{1,0:T(8,128)(2,1)S(1)}, bf16[2560,128]{1,0:T(8,128)(2,1)S(1)}, u32[]{:S(2)}, u32[]{:S(2)}) collective-permute-start(bf16[2560,128]{1,0:T(8,128)(2,1)S(1)} %first_pack.1), channel_id=1, source_target_pairs={{0,256},{16,272},{32,288},{48,304},{64,320},{80,336},{96,352},{112... | collective-permute-start | bytes 1966088 | tf_op jit(solution)/shard_map/ppermute | solution.py:332
  15.9 18.4 %collective-permute-start = (bf16[128,640]{1,0:T(8,128)(2,1)S(1)}, bf16[128,640]{1,0:T(8,128)(2,1)S(1)}, u32[]{:S(2)}, u32[]{:S(2)}) collective-permute-start(bf16[128,640]{1,0:T(8,128)(2,1)S(1)} %bitcast.8), channel_id=1, source_target_pairs={{0,16},{16,0},{32,48},{48,32},{64,80},{80,64},{96,112},{112,96},{1... | collective-permute-start | bytes 491528 | tf_op jit(solution)/shard_map/ppermute | solution.py:331
  34.3 0.7 copy-start.2
  65.5 28.4 %collective-permute-start.2 = (f32[8,1,1152]{2,1,0:T(1,128)S(1)}, f32[8,1,1152]{2,1,0:T(1,128)S(1)}, u32[]{:S(2)}, u32[]{:S(2)}) collective-permute-start(f32[8,1,1152]{2,1,0:T(1,128)S(1)} %edge_sums.1), channel_id=1, source_target_pairs={{0,240},{16,0},{32,16},{48,32},{64,48},{80,64},{96,80},{112,96},{1... | collective-permute-start | bytes 110600 | tf_op jit(solution)/shard_map/ppermute | solution.py:342

commit v4 on v3

--- a/solution.py
+++ b/solution.py
@@ -331,12 +331,12 @@
     other = lax.ppermute(shard, "tm", [(i, i ^ 1) for i in range(tm)])
     got = lax.ppermute(first_pack(place, waveform), "tm", partner)
 
-    def spread(lags):
-        return lax.all_to_all(lag_pack(lags), "tm", 0, 0, axis_index_groups=plane)
-
-    own = spread(shard)
-    other, got = lax.optimization_barrier((other, got))
-    oth = spread(other)
+    def exchange(copies):
+        return lax.all_to_all(copies, "tm", 0, 0, axis_index_groups=plane)
+
+    own = lax.cond(me // tm == 0, exchange, lambda copies: copies, lag_pack(shard))
+    other, got, own = lax.optimization_barrier((other, got, own))
+    oth = exchange(lag_pack(other))
 
     edges = edge_sums(place, waveform, got, own, oth)
     edges = lax.ppermute(edges, "tm", [(i, i - 1 if i % 8 else (i ^ 8) + 7) for i in range(tm)])

time: 123 us -> 120 us (0.976)
  blocking collectives: 46.4 us -> 66.3 us
  starting transfers between devices: 47.6 us -> 30.4 us
  waiting for transfers between devices: 7.27 us -> 0.01 us
  local copies, waits for them, and re-layouts: 0.76 us -> 2.15 us
    all_to_all x1 -> x2, blocking collectives: 19.9 us -> 42.9 us  [exchange(): return lax.all_to_all(copies, 'tm', 0, 0, axis_index_groups=plane)]
    ppermute x1, starting transfers between devices: 19.6 us -> 9.48 us  [local(): lax.ppermute(edges, 'tm', [(i, i - 1 if i % 8 else (i ^ 8) + 7) for i in...]
    all_to_all x1 -> x0, starting transfers between devices: 7.72 us -> none  [spread(): return lax.all_to_all(lag_pack(lags), 'tm', 0, 0, axis_index_groups=plane)]
    ppermute x1, waiting for transfers between devices: 4.26 us -> 0.01 us  [local(): got = lax.ppermute(first_pack(place, waveform), 'tm', partner)]
    all_to_all x1, blocking collectives: 26.5 us -> 23.4 us  [local(): parts = lax.all_to_all(parts, ('tm', 'chan'), 0, 0, axis_index_groups=pairs)]
    ppermute x1, waiting for transfers between devices: 3 us -> 0.01 us  [local(): other = lax.ppermute(shard, 'tm', [(i, i ^ 1) for i in range(tm)])]
    unnamed x6 -> x8, local copies, waits for them, and re-layouts: 0.69 us -> 1.99 us
  transfers between devices with their start and end apart: 4 -> 3, of which waited for: 2 -> 0; matrix products, arithmetic and copies ran while one was open for 0% -> 0% of each run, Pallas kernels for 10% -> 10%
where the time goes in v4:
time: 120 us
  blocking collectives  66.3 us (55%)
  starting transfers between devices  30.4 us (25%)
  Pallas kernels  20.6 us (17%)
  local copies, waits for them, and re-layouts  2.15 us (2%)
    all_to_all x2, blocking collectives, exchange(): return lax.all_to_all(copies, 'tm', 0, 0, axis_index_groups=plane)  42.9 us
    all_to_all x1, blocking collectives, local(): parts = lax.all_to_all(parts, ('tm', 'chan'), 0, 0, axis_index_groups=pairs)  23.4 us
    ppermute x1, starting transfers between devices, local(): other = lax.ppermute(shard, 'tm', [(i, i ^ 1) for i in range(tm)])  15.4 us
    ppermute x1, starting transfers between devices, local(): lax.ppermute(edges, 'tm', [(i, i - 1 if i % 8 else (i ^ 8) + 7) for i in...  9.48 us
    pallas_call x1, Pallas kernels, main_sums(): pl.pallas_call(main_kernel, out_shape=jax.ShapeDtypeStruct((32, 1, 1152),...  8.79 us
    ppermute x1, starting transfers between devices, local(): got = lax.ppermute(first_pack(place, waveform), 'tm', partner)  5.48 us
    pallas_call x2, Pallas kernels, lag_pack(): pl.pallas_call(lag_pack_kernel, out_shape=jax.ShapeDtypeStruct((16, 320,...  5.42 us
    pallas_call x1, Pallas kernels, edge_sums(): pl.pallas_call(edge_kernel, out_shape=jax.ShapeDtypeStruct((8, 1, 1152),...  3.89 us
  transfers between devices with their start and end apart: 3, of which 0 were waited for; matrix products, arithmetic and copies ran while one was open for 0% of the time, Pallas kernels for 10%

profile of v4, /device:TPU:1, one launch (start us, length us, event | category | flops | bytes accessed | tf_op | source)
XLA Modules:
  0.0 119.9 jit_solution(14266054798959319940)
XLA Ops:
  0.0 0.1 pad_add_fusion.place
  0.1 0.0 copy-start
  0.1 1.3 %copy-done = bf16[1024,640]{1,0:T(8,128)(2,1)S(1)} copy-done((bf16[1024,640]{1,0:T(8,128)(2,1)S(1)}, bf16[1024,640]{1,0:T(8,128)(2,1)}, u32[]{:S(2)}) %copy-start) | copy-done | bytes 1310744
  1.4 0.0 copy-start.2
  1.4 0.8 first_pack.1
  2.2 5.5 %collective-permute-start.1 = (bf16[2560,128]{1,0:T(8,128)(2,1)S(1)}, bf16[2560,128]{1,0:T(8,128)(2,1)S(1)}, u32[]{:S(2)}, u32[]{:S(2)}) collective-permute-start(bf16[2560,128]{1,0:T(8,128)(2,1)S(1)} %first_pack.1), channel_id=1, source_target_pairs={{0,256},{16,272},{32,288},{48,304},{64,320},{80,336},{96,352},{112... | collective-permute-start | bytes 1966088 | tf_op jit(solution)/shard_map/ppermute | solution.py:332
  7.7 0.0 copy-done.2
  7.7 15.4 %collective-permute-start = (bf16[128,640]{1,0:T(8,128)(2,1)S(1)}, bf16[128,640]{1,0:T(8,128)(2,1)S(1)}, u32[]{:S(2)}, u32[]{:S(2)}) collective-permute-start(bf16[128,640]{1,0:T(8,128)(2,1)S(1)} %bitcast.8), channel_id=1, source_target_pairs={{0,16},{16,0},{32,48},{48,32},{64,80},{80,64},{96,112},{112,96},{1... | collective-permute-start | bytes 491528 | tf_op jit(solution)/shard_map/ppermute | solution.py:331
  23.1 3.0 %lag_pack.2 = bf16[16,320,128]{2,1,0:T(8,128)(2,1)S(1)} custom-call(bf16[128,640]{1,0:T(8,128)(2,1)} %bitcast.7), custom_call_target="tpu_custom_call" | custom-call | flops 2000000 | bytes 1500000 | tf_op jit(solution)/shard_map/lag_pack/pallas_call | solution.py:86
  26.2 22.5 %conditional.1 = (bf16[16,320,128]{2,1,0:T(8,128)(2,1)S(1)}) conditional(s32[]{:T(128)} %convert_element_type.6, bf16[16,320,128]{2,1,0:T(8,128)(2,1)S(1)} %lag_pack.2, bf16[16,320,128]{2,1,0:T(8,128)(2,1)S(1)} %lag_pack.2), branch_computations={%region_0.1_spmd, %region_1.2_spmd} | conditional | bytes 5242888 | solution.py:337
  26.2 0.1 copy.5
  26.3 22.4 %all_to_all.14 = bf16[16,320,128]{2,1,0:T(8,128)(2,1)S(1)} all-to-all(bf16[16,320,128]{2,1,0:T(8,128)(2,1)S(1)} %copy.5), channel_id=1, replica_groups={{0,32,64,96,128,160,192,224,256,288,320,352,384,416,448,480},{16,48,80,..., dimensions={0} | all-to-all | bytes 2621440 | tf_op jit(solution)/shard_map/cond/branch_1_fun/all_to_all | solution.py:335
  48.7 0.0 collective-permute-done.lags
  48.7 0.0 copy-start.3
  48.7 0.0 collective-permute-done.1.got
  48.7 0.7 copy-done.3
  49.4 2.4 %lag_pack.3 = bf16[16,320,128]{2,1,0:T(8,128)(2,1)} custom-call(bf16[128,640]{1,0:T(8,128)(2,1)} %copy-done.3), custom_call_target="tpu_custom_call" | custom-call | flops 2000000 | bytes 1500000 | tf_op jit(solution)/shard_map/lag_pack/pallas_call | solution.py:86
  51.8 0.0 copy-start.1
  51.8 20.5 %all_to_all.15.oth = bf16[16,320,128]{2,1,0:T(8,128)(2,1)S(1)} all-to-all(bf16[16,320,128]{2,1,0:T(8,128)(2,1)} %lag_pack.3), channel_id=1, replica_groups={{0,32,64,96,128,160,192,224,256,288,320,352,384,416,448,480},{16,48,80,..., dimensions={0} | all-to-all | bytes 2621440 | tf_op jit(solution)/shard_map/all_to_all | solution.py:335
  72.3 0.0 copy-done.1
  72.3 3.9 %edge_sums.1 = f32[8,1,1152]{2,1,0:T(1,128)S(1)} custom-call(s32[3]{0:T(128)S(1)} %pad_add_fusion.place, bf16[1024,640]{1,0:T(8,128)(2,1)S(1)} %copy-done.1, bf16[2560,128]{1,0:T(8,128)(2,1)S(1)} %collective-permute-done.1.got, bf16[16,320,128]{2,1,0:T(8,128)(2,1)S(1)} %get-tuple-element.16.own, bf16[16,320,128]{2,1,0:T(8,128)(2,1)S(1)} %all_to_all.15.oth), custom_call_target="tpu_custom_call" | custom-call | flops 1400000000 | bytes 3200000 | tf_op jit(solution)/shard_map/edge_sums/pallas_call | solution.py:272
  76.2 9.5 %collective-permute-start.2 = (f32[8,1,1152]{2,1,0:T(1,128)S(1)}, f32[8,1,1152]{2,1,0:T(1,128)S(1)}, u32[]{:S(2)}, u32[]{:S(2)}) collective-permute-start(f32[8,1,1152]{2,1,0:T(1,128)S(1)} %edge_sums.1), channel_id=1, source_target_pairs={{0,240},{16,0},{32,16},{48,32},{64,48},{80,64},{96,80},{112,96},{1... | collective-permute-start | bytes 110600 | tf_op jit(solution)/shard_map/ppermute | solution.py:342
  85.7 8.8 %main_sums.1 = f32[32,1,1152]{2,1,0:T(1,128)S(1)} custom-call(s32[3]{0:T(128)S(1)} %pad_add_fusion.place, bf16[1024,640]{1,0:T(8,128)(2,1)S(1)} %copy-done.1, bf16[2560,128]{1,0:T(8,128)(2,1)S(1)} %collective-permute-done.1.got, bf16[16,320,128]{2,1,0:T(8,128)(2,1)S(1)} %get-tuple-element.16.own, bf16[16,320,128]{2,1,0:T(8,128)(2,1)S(1)} %all_to_all.15.oth), custom_call_target="tpu_custom_call" | custom-call | flops 5500000256 | bytes 5000000 | tf_op jit(solution)/shard_map/main_sums/pallas_call | solution.py:286
  94.5 0.0 collective-permute-done.2
  94.5 0.1 pad.4
  94.6 0.2 bitcast_add_fusion
  94.8 23.4 %all_to_all.16.parts = f32[32,1,1152]{2,1,0:T(1,128)} all-to-all(f32[32,1,1152]{2,1,0:T(1,128)S(1)} %bitcast_add_fusion), channel_id=1, replica_groups={{0,1,2,3,4,5,6,7,8,9,10,11,12,13,14,15,256,257,258,259,260,261,262,263,..., dimensions={0} | all-to-all | bytes 294912 | tf_op jit(solution)/shard_map/all_to_all | solution.py:348
  118.2 1.7 %finish.1 = f32[16,64]{1,0:T(8,128)} custom-call(f32[32,1,1152]{2,1,0:T(1,128)} %all_to_all.16.parts), custom_call_target="tpu_custom_call" | custom-call | tf_op jit(solution)/shard_map/finish/pallas_call | solution.py:311
Async XLA Ops:
  0.1 1.3 %copy-start = (bf16[1024,640]{1,0:T(8,128)(2,1)S(1)}, bf16[1024,640]{1,0:T(8,128)(2,1)}, u32[]{:S(2)}) copy-start(bf16[1024,640]{1,0:T(8,128)(2,1)} %x.7) | copy-start | bytes 3932164
  1.4 6.3 %copy-start.2 = (bf16[16,8,640]{2,1,0:T(8,128)(2,1)S(1)}, bf16[16,8,640]{2,1,0:T(8,128)(2,1)}, u32[]{:S(2)}) copy-start(bf16[16,8,640]{2,1,0:T(8,128)(2,1)} %param.5) | copy-start | bytes 491524
  2.2 46.5 %collective-permute-start.1 = (bf16[2560,128]{1,0:T(8,128)(2,1)S(1)}, bf16[2560,128]{1,0:T(8,128)(2,1)S(1)}, u32[]{:S(2)}, u32[]{:S(2)}) collective-permute-start(bf16[2560,128]{1,0:T(8,128)(2,1)S(1)} %first_pack.1), channel_id=1, source_target_pairs={{0,256},{16,272},{32,288},{48,304},{64,320},{80,336},{96,352},{112... | collective-permute-start | bytes 1966088 | tf_op jit(solution)/shard_map/ppermute | solution.py:332
  7.7 41.0 %collective-permute-start = (bf16[128,640]{1,0:T(8,128)(2,1)S(1)}, bf16[128,640]{1,0:T(8,128)(2,1)S(1)}, u32[]{:S(2)}, u32[]{:S(2)}) collective-permute-start(bf16[128,640]{1,0:T(8,128)(2,1)S(1)} %bitcast.8), channel_id=1, source_target_pairs={{0,16},{16,0},{32,48},{48,32},{64,80},{80,64},{96,112},{112,96},{1... | collective-permute-start | bytes 491528 | tf_op jit(solution)/shard_map/ppermute | solution.py:331
  48.7 0.7 copy-start.3
  51.8 20.5 %copy-start.1 = (bf16[1024,640]{1,0:T(8,128)(2,1)S(1)}, bf16[1024,640]{1,0:T(8,128)(2,1)}, u32[]{:S(2)}) copy-start(bf16[1024,640]{1,0:T(8,128)(2,1)} %x.7) | copy-start | bytes 3932164
  76.2 18.3 %collective-permute-start.2 = (f32[8,1,1152]{2,1,0:T(1,128)S(1)}, f32[8,1,1152]{2,1,0:T(1,128)S(1)}, u32[]{:S(2)}, u32[]{:S(2)}) collective-permute-start(f32[8,1,1152]{2,1,0:T(1,128)S(1)} %edge_sums.1), channel_id=1, source_target_pairs={{0,240},{16,0},{32,16},{48,32},{64,48},{80,64},{96,80},{112,96},{1... | collective-permute-start | bytes 110600 | tf_op jit(solution)/shard_map/ppermute | solution.py:342

commit v5 on v4

--- a/solution.py
+++ b/solution.py
@@ -39,44 +39,44 @@
     return jnp.where(low_lanes(), swap(v[:n]), v[n:])
 
 
-def pack_half(v, half, upper):
-    return [
-        jnp.where(upper, v[:, 256:384], v[:, 0:128]),
-        jnp.where(upper, v[:, 384:512], v[:, 128:256]),
-        jnp.where(upper, pack_rest(v[:, 512:640], 1), pack_rest(v[:, 512:640], 0)),
+def first_pack_kernel(place, x, send, rest, sems):
+    other = 1 - place[1]
+    moves = [
+        pltpu.make_async_copy(x.at[:, pl.ds(512, 128)], rest, sems.at[0]),
+        pltpu.make_async_copy(x.at[:, lanes_of(other, 0)], send.at[pl.ds(0, ROWS)], sems.at[1]),
+        pltpu.make_async_copy(x.at[:, lanes_of(other, 1)], send.at[pl.ds(ROWS, ROWS)], sems.at[2]),
     ]
-
-
-def first_pack_kernel(place, x, send):
-    at = 0
-    for part in pack_half(x[...], None, place[1] == 0):
-        send[at : at + part.shape[0]] = part
-        at += part.shape[0]
-
-
-def lag_pack_kernel(lags, copies, packed, sems):
+    for move in moves:
+        move.start()
+    moves[0].wait()
+    v = rest[...]
+    send[2 * ROWS :] = jnp.where(other == 1, pack_rest(v, 1), pack_rest(v, 0))
+    for move in moves[1:]:
+        move.wait()
+
+
+def lag_pack_kernel(lags, copies):
     i = lax.broadcasted_iota(jnp.int32, (K * SUB, K * SUB), 0)
     j = lax.broadcasted_iota(jnp.int32, (K * SUB, K * SUB), 1)
     order = (i // SUB * SUB + (SUB - 1 - i % SUB) == j).astype(BF16)
     v = lax.dot_general(order, lags[...], NN, preferred_element_type=jnp.float32).astype(BF16)
     for half in range(2):
-        packed[half, 0:128] = v[:, 256 * half : 256 * half + 128]
-        packed[half, 128:256] = v[:, 256 * half + 128 : 256 * half + 256]
-        packed[half, 256:320] = pack_rest(v[:, 512:640], half)
-    moves = [pltpu.make_async_copy(packed.at[p // 8], copies.at[p], sems.at[p]) for p in range(16)]
-    for move in moves:
-        move.start()
-    for move in moves:
-        move.wait()
+        first, second = v[:, 256 * half : 256 * half + 128], v[:, 256 * half + 128 : 256 * half + 256]
+        rest = pack_rest(v[:, 512:640], half)
+        for p in range(8 * half, 8 * half + 8):
+            copies[p, 0:128] = first
+            copies[p, 128:256] = second
+            copies[p, 256:320] = rest
 
 
 def first_pack(place, x):
     return pl.pallas_call(
         first_pack_kernel,
         out_shape=jax.ShapeDtypeStruct((ROWS * 5 // 2, 128), BF16),
-        in_specs=[SMEM, VMEM],
-        out_specs=VMEM,
-        compiler_params=pltpu.CompilerParams(vmem_limit_bytes=16 * 2**20),
+        in_specs=[SMEM, ANY],
+        out_specs=VMEM,
+        scratch_shapes=[pltpu.VMEM((ROWS, 128), BF16), pltpu.SemaphoreType.DMA((3,))],
+        compiler_params=pltpu.CompilerParams(vmem_limit_bytes=8 * 2**20),
         cost_estimate=pl.CostEstimate(flops=2_000_000, bytes_accessed=2_000_000, transcendentals=0),
         name="first_pack",
     )(place, x)
@@ -87,8 +87,8 @@
         lag_pack_kernel,
         out_shape=jax.ShapeDtypeStruct((16, 320, 128), BF16),
         in_specs=[VMEM],
-        out_specs=ANY,
-        scratch_shapes=[pltpu.VMEM((2, 320, 128), BF16), pltpu.SemaphoreType.DMA((16,))],
+        out_specs=VMEM,
+        compiler_params=pltpu.CompilerParams(vmem_limit_bytes=8 * 2**20),
         cost_estimate=pl.CostEstimate(flops=2_000_000, bytes_accessed=1_500_000, transcendentals=0),
         name="lag_pack",
     )(lags)
@@ -185,29 +185,26 @@
     x2[b, n - 16 : n] = jnp.where(low_lanes(), left[n - 16 : n], jnp.zeros((16, 128), BF16))
 
 
-def fetch(x, got, own, oth, half, rows, at, xm, mine, his, lo_lags, hi_lags, sems):
+def fetch(x, got, half, rows, at, xm, mine, his, sems):
     first = [
         pltpu.make_async_copy(x.at[pl.ds(0, rows), pl.ds(512, 128)], mine, sems.at[0]),
         pltpu.make_async_copy(got.at[pl.ds(2 * ROWS, his.shape[0])], his, sems.at[1]),
     ]
-    second = [
-        pltpu.make_async_copy(own, lo_lags, sems.at[2]),
-        pltpu.make_async_copy(oth, hi_lags, sems.at[3]),
-    ]
+    second = []
     for c in range(2):
         lanes, body = pl.ds(128 * c, 128), pl.ds(at, rows)
         second += [
-            pltpu.make_async_copy(x.at[pl.ds(0, rows), lanes_of(half, c)], xm.at[0, body, lanes], sems.at[4 + c]),
-            pltpu.make_async_copy(got.at[pl.ds(ROWS * c, rows)], xm.at[1, body, lanes], sems.at[6 + c]),
+            pltpu.make_async_copy(x.at[pl.ds(0, rows), lanes_of(half, c)], xm.at[0, body, lanes], sems.at[2 + c]),
+            pltpu.make_async_copy(got.at[pl.ds(ROWS * c, rows)], xm.at[1, body, lanes], sems.at[4 + c]),
         ]
     for move in first + second:
         move.start()
     return first, second
 
 
-def edge_kernel(place, x, got, own, oth, edges, xm, x2, q, mine, his, lo_lags, hi_lags, sums, sems):
+def edge_kernel(place, x, got, own, oth, edges, xm, x2, q, mine, his, sums, sems):
     z, half = place[0], place[1]
-    first, second = fetch(x, got, own, oth, half, RIM, RIM, xm, mine, his, lo_lags, hi_lags, sems)
+    first, second = fetch(x, got, half, RIM, RIM, xm, mine, his, sems)
     for move in first:
         move.wait()
     for b in range(2):
@@ -221,7 +218,7 @@
         lay_out_rest(x2, b, left, right, RIM, 0)
     for move in second:
         move.wait()
-    sum_lags(xm, x2, q, lo_lags, hi_lags, EDGE_USED, False)
+    sum_lags(xm, x2, q, own, oth, EDGE_USED, False)
     for b in range(2):
         stack = sum_fine_lags(q, b, EDGE_SPAN, EDGE_USED, z)
         de = window_energy(xm, x2, b, 2 * RIM)
@@ -233,9 +230,9 @@
     edges[4:8] = jnp.where(turn, jnp.zeros_like(high), high)
 
 
-def main_kernel(place, x, got, own, oth, out, xm, x2, q, mine, his, lo_lags, hi_lags, sems):
+def main_kernel(place, x, got, own, oth, out, xm, x2, q, mine, his, sems):
     z, half = place[0], place[1]
-    first, second = fetch(x, got, own, oth, half, ROWS, 0, xm, mine, his, lo_lags, hi_lags, sems)
+    first, second = fetch(x, got, half, ROWS, 0, xm, mine, his, sems)
     for move in first:
         move.wait()
     for b in range(2):
@@ -249,7 +246,7 @@
         lay_out_rest(x2, b, left, right, 0, RIM)
     for move in second:
         move.wait()
-    te_row = sum_lags(xm, x2, q, lo_lags, hi_lags, USED, True)
+    te_row = sum_lags(xm, x2, q, own, oth, USED, True)
     for b in range(2):
         stack = sum_fine_lags(q, b, SPAN, USED, z)
         de = window_energy(xm, x2, b, ROWS + RIM)
@@ -263,8 +260,6 @@
         pltpu.VMEM((2, span, 2 * K * SUB), jnp.float32),
         pltpu.VMEM((rows, 128), BF16),
         pltpu.VMEM((his_rows, 128), BF16),
-        pltpu.VMEM((16, 320, 128), BF16),
-        pltpu.VMEM((16, 320, 128), BF16),
     ]
 
 
@@ -272,11 +267,11 @@
     return pl.pallas_call(
         edge_kernel,
         out_shape=jax.ShapeDtypeStruct((8, 1, 1152), jnp.float32),
-        in_specs=[SMEM] + [ANY] * 4,
+        in_specs=[SMEM, ANY, ANY, VMEM, VMEM],
         out_specs=VMEM,
         scratch_shapes=scratch(RIM, EDGE_SPAN, RIM)
-        + [pltpu.VMEM((8, 1, 1152), jnp.float32), pltpu.SemaphoreType.DMA((8,))],
-        compiler_params=pltpu.CompilerParams(vmem_limit_bytes=32 * 2**20),
+        + [pltpu.VMEM((8, 1, 1152), jnp.float32), pltpu.SemaphoreType.DMA((6,))],
+        compiler_params=pltpu.CompilerParams(vmem_limit_bytes=20 * 2**20),
         cost_estimate=pl.CostEstimate(flops=1_400_000_000, bytes_accessed=3_200_000, transcendentals=0),
         name="edge_sums",
     )(*args)
@@ -286,9 +281,9 @@
     return pl.pallas_call(
         main_kernel,
         out_shape=jax.ShapeDtypeStruct((32, 1, 1152), jnp.float32),
-        in_specs=[SMEM] + [ANY] * 4,
-        out_specs=VMEM,
-        scratch_shapes=scratch(ROWS, SPAN, ROWS // 2) + [pltpu.SemaphoreType.DMA((8,))],
+        in_specs=[SMEM, ANY, ANY, VMEM, VMEM],
+        out_specs=VMEM,
+        scratch_shapes=scratch(ROWS, SPAN, ROWS // 2) + [pltpu.SemaphoreType.DMA((6,))],
         compiler_params=pltpu.CompilerParams(vmem_limit_bytes=48 * 2**20),
         cost_estimate=pl.CostEstimate(flops=5_500_000_000, bytes_accessed=5_000_000, transcendentals=0),
         name="main_sums",
@@ -313,6 +308,7 @@
         out_shape=jax.ShapeDtypeStruct((K, 64), jnp.float32),
         in_specs=[VMEM],
         out_specs=VMEM,
+        compiler_params=pltpu.CompilerParams(vmem_limit_bytes=4 * 2**20),
         name="finish",
     )(parts)
 

time: 120 us -> 117 us (0.975)
  Pallas kernels: 20.6 us -> 14.6 us
  starting transfers between devices: 30.4 us -> 33.1 us
    pallas_call x2, Pallas kernels: 5.42 us -> 0.6 us  [lag_pack(): pl.pallas_call(lag_pack_kernel, out_shape=jax.ShapeDtypeStruct((16, 320,...]
    ppermute x1, starting transfers between devices: 9.48 us -> 12.2 us  [local(): lax.ppermute(edges, 'tm', [(i, i - 1 if i % 8 else (i ^ 8) + 7) for i in...]
  transfers between devices with their start and end apart: 3 -> 3, of which waited for: 0 -> 0; matrix products, arithmetic and copies ran while one was open for 0% -> 0% of each run, Pallas kernels for 10% -> 8%
where the time goes in v5:
time: 117 us; the launch traced here: 116 us
  blocking collectives  66.8 us (57%)
  starting transfers between devices  33.1 us (28%)
  Pallas kernels  14.6 us (12%)
  local copies, waits for them, and re-layouts  1.49 us (1%)
    all_to_all x2, blocking collectives, exchange(): return lax.all_to_all(copies, 'tm', 0, 0, axis_index_groups=plane)  42.7 us
    all_to_all x1, blocking collectives, local(): parts = lax.all_to_all(parts, ('tm', 'chan'), 0, 0, axis_index_groups=pairs)  24.1 us
    ppermute x1, starting transfers between devices, local(): other = lax.ppermute(shard, 'tm', [(i, i ^ 1) for i in range(tm)])  15.4 us
    ppermute x1, starting transfers between devices, local(): lax.ppermute(edges, 'tm', [(i, i - 1 if i % 8 else (i ^ 8) + 7) for i in...  12.2 us
    pallas_call x1, Pallas kernels, main_sums(): pl.pallas_call(main_kernel, out_shape=jax.ShapeDtypeStruct((32, 1, 1152),...  8.65 us
    ppermute x1, starting transfers between devices, local(): got = lax.ppermute(first_pack(place, waveform), 'tm', partner)  5.48 us
    pallas_call x1, Pallas kernels, edge_sums(): pl.pallas_call(edge_kernel, out_shape=jax.ShapeDtypeStruct((8, 1, 1152),...  3.75 us
  transfers between devices with their start and end apart: 3, of which 0 were waited for; matrix products, arithmetic and copies ran while one was open for 0% of the time, Pallas kernels for 8%

profile of v5, /device:TPU:1, one launch (start us, length us, event | category | flops | bytes accessed | tf_op | source)
XLA Modules:
  0.0 116.5 jit_solution(17336335904389309033)
XLA Ops:
  0.0 0.1 pad_add_fusion.place
  0.1 0.0 copy-start
  0.1 1.3 %copy-done = bf16[1024,640]{1,0:T(8,128)(2,1)S(1)} copy-done((bf16[1024,640]{1,0:T(8,128)(2,1)S(1)}, bf16[1024,640]{1,0:T(8,128)(2,1)}, u32[]{:S(2)}) %copy-start) | copy-done | bytes 1310744
  1.4 0.0 copy-start.2
  1.4 0.9 first_pack.1
  2.3 5.5 %collective-permute-start.1 = (bf16[2560,128]{1,0:T(8,128)(2,1)S(1)}, bf16[2560,128]{1,0:T(8,128)(2,1)S(1)}, u32[]{:S(2)}, u32[]{:S(2)}) collective-permute-start(bf16[2560,128]{1,0:T(8,128)(2,1)S(1)} %first_pack.1), channel_id=1, source_target_pairs={{0,256},{16,272},{32,288},{48,304},{64,320},{80,336},{96,352},{112... | collective-permute-start | bytes 1966088 | tf_op jit(solution)/shard_map/ppermute | solution.py:328
  7.7 0.0 copy-done.2
  7.8 15.4 %collective-permute-start = (bf16[128,640]{1,0:T(8,128)(2,1)S(1)}, bf16[128,640]{1,0:T(8,128)(2,1)S(1)}, u32[]{:S(2)}, u32[]{:S(2)}) collective-permute-start(bf16[128,640]{1,0:T(8,128)(2,1)S(1)} %bitcast.7), channel_id=1, source_target_pairs={{0,16},{16,0},{32,48},{48,32},{64,80},{80,64},{96,112},{112,96},{1... | collective-permute-start | bytes 491528 | tf_op jit(solution)/shard_map/ppermute | solution.py:327
  23.2 0.3 lag_pack.2
  23.5 22.5 %conditional.1 = (bf16[16,320,128]{2,1,0:T(8,128)(2,1)S(1)}) conditional(s32[]{:T(128)} %convert_element_type.6, bf16[16,320,128]{2,1,0:T(8,128)(2,1)S(1)} %lag_pack.2, bf16[16,320,128]{2,1,0:T(8,128)(2,1)S(1)} %lag_pack.2), branch_computations={%region_0.1_spmd, %region_1.2_spmd} | conditional | bytes 5242888 | solution.py:333
  23.5 0.1 copy.5
  23.6 22.4 %all_to_all.14 = bf16[16,320,128]{2,1,0:T(8,128)(2,1)S(1)} all-to-all(bf16[16,320,128]{2,1,0:T(8,128)(2,1)S(1)} %copy.5), channel_id=1, replica_groups={{0,32,64,96,128,160,192,224,256,288,320,352,384,416,448,480},{16,48,80,..., dimensions={0} | all-to-all | bytes 2621440 | tf_op jit(solution)/shard_map/cond/branch_1_fun/all_to_all | solution.py:331
  46.0 0.0 collective-permute-done.lags
  46.0 0.0 collective-permute-done.1.got
  46.0 0.3 lag_pack.3
  46.4 0.0 copy-start.1
  46.4 20.3 %all_to_all.15.oth = bf16[16,320,128]{2,1,0:T(8,128)(2,1)S(1)} all-to-all(bf16[16,320,128]{2,1,0:T(8,128)(2,1)S(1)} %lag_pack.3), channel_id=1, replica_groups={{0,32,64,96,128,160,192,224,256,288,320,352,384,416,448,480},{16,48,80,..., dimensions={0} | all-to-all | bytes 2621440 | tf_op jit(solution)/shard_map/all_to_all | solution.py:331
  66.7 0.0 copy-done.1
  66.7 3.8 %edge_sums.1 = f32[8,1,1152]{2,1,0:T(1,128)S(1)} custom-call(s32[3]{0:T(128)S(1)} %pad_add_fusion.place, bf16[1024,640]{1,0:T(8,128)(2,1)S(1)} %copy-done.1, bf16[2560,128]{1,0:T(8,128)(2,1)S(1)} %collective-permute-done.1.got, bf16[16,320,128]{2,1,0:T(8,128)(2,1)S(1)} %get-tuple-element.16.own, bf16[16,320,128]{2,1,0:T(8,128)(2,1)S(1)} %all_to_all.15.oth), custom_call_target="tpu_custom_call" | custom-call | flops 1400000000 | bytes 3200000 | tf_op jit(solution)/shard_map/edge_sums/pallas_call | solution.py:267
  70.5 12.2 %collective-permute-start.2 = (f32[8,1,1152]{2,1,0:T(1,128)S(1)}, f32[8,1,1152]{2,1,0:T(1,128)S(1)}, u32[]{:S(2)}, u32[]{:S(2)}) collective-permute-start(f32[8,1,1152]{2,1,0:T(1,128)S(1)} %edge_sums.1), channel_id=1, source_target_pairs={{0,240},{16,0},{32,16},{48,32},{64,48},{80,64},{96,80},{112,96},{1... | collective-permute-start | bytes 110600 | tf_op jit(solution)/shard_map/ppermute | solution.py:338
  82.6 8.6 %main_sums.1 = f32[32,1,1152]{2,1,0:T(1,128)S(1)} custom-call(s32[3]{0:T(128)S(1)} %pad_add_fusion.place, bf16[1024,640]{1,0:T(8,128)(2,1)S(1)} %copy-done.1, bf16[2560,128]{1,0:T(8,128)(2,1)S(1)} %collective-permute-done.1.got, bf16[16,320,128]{2,1,0:T(8,128)(2,1)S(1)} %get-tuple-element.16.own, bf16[16,320,128]{2,1,0:T(8,128)(2,1)S(1)} %all_to_all.15.oth), custom_call_target="tpu_custom_call" | custom-call | flops 5500000256 | bytes 5000000 | tf_op jit(solution)/shard_map/main_sums/pallas_call | solution.py:281
  91.3 0.0 collective-permute-done.2
  91.3 0.1 pad.4
  91.4 0.2 bitcast_add_fusion
  91.6 24.1 %all_to_all.16.parts = f32[32,1,1152]{2,1,0:T(1,128)S(1)} all-to-all(f32[32,1,1152]{2,1,0:T(1,128)S(1)} %bitcast_add_fusion), channel_id=1, replica_groups={{0,1,2,3,4,5,6,7,8,9,10,11,12,13,14,15,256,257,258,259,260,261,262,263,..., dimensions={0} | all-to-all | bytes 294912 | tf_op jit(solution)/shard_map/all_to_all | solution.py:344
  115.7 0.8 finish.1
Async XLA Ops:
  0.1 1.3 %copy-start = (bf16[1024,640]{1,0:T(8,128)(2,1)S(1)}, bf16[1024,640]{1,0:T(8,128)(2,1)}, u32[]{:S(2)}) copy-start(bf16[1024,640]{1,0:T(8,128)(2,1)} %x.7) | copy-start | bytes 3932164
  1.4 6.4 %copy-start.2 = (bf16[16,8,640]{2,1,0:T(8,128)(2,1)S(1)}, bf16[16,8,640]{2,1,0:T(8,128)(2,1)}, u32[]{:S(2)}) copy-start(bf16[16,8,640]{2,1,0:T(8,128)(2,1)} %param.5) | copy-start | bytes 491524
  2.3 43.8 %collective-permute-start.1 = (bf16[2560,128]{1,0:T(8,128)(2,1)S(1)}, bf16[2560,128]{1,0:T(8,128)(2,1)S(1)}, u32[]{:S(2)}, u32[]{:S(2)}) collective-permute-start(bf16[2560,128]{1,0:T(8,128)(2,1)S(1)} %first_pack.1), channel_id=1, source_target_pairs={{0,256},{16,272},{32,288},{48,304},{64,320},{80,336},{96,352},{112... | collective-permute-start | bytes 1966088 | tf_op jit(solution)/shard_map/ppermute | solution.py:328
  7.8 38.3 %collective-permute-start = (bf16[128,640]{1,0:T(8,128)(2,1)S(1)}, bf16[128,640]{1,0:T(8,128)(2,1)S(1)}, u32[]{:S(2)}, u32[]{:S(2)}) collective-permute-start(bf16[128,640]{1,0:T(8,128)(2,1)S(1)} %bitcast.7), channel_id=1, source_target_pairs={{0,16},{16,0},{32,48},{48,32},{64,80},{80,64},{96,112},{112,96},{1... | collective-permute-start | bytes 491528 | tf_op jit(solution)/shard_map/ppermute | solution.py:327
  46.4 20.3 %copy-start.1 = (bf16[1024,640]{1,0:T(8,128)(2,1)S(1)}, bf16[1024,640]{1,0:T(8,128)(2,1)}, u32[]{:S(2)}) copy-start(bf16[1024,640]{1,0:T(8,128)(2,1)} %x.7) | copy-start | bytes 3932164
  70.5 20.8 %collective-permute-start.2 = (f32[8,1,1152]{2,1,0:T(1,128)S(1)}, f32[8,1,1152]{2,1,0:T(1,128)S(1)}, u32[]{:S(2)}, u32[]{:S(2)}) collective-permute-start(f32[8,1,1152]{2,1,0:T(1,128)S(1)} %edge_sums.1), channel_id=1, source_target_pairs={{0,240},{16,0},{32,16},{48,32},{64,48},{80,64},{96,80},{112,96},{1... | collective-permute-start | bytes 110600 | tf_op jit(solution)/shard_map/ppermute | solution.py:338

commit v6 on v5

--- a/solution.py
+++ b/solution.py
@@ -63,10 +63,11 @@
     for half in range(2):
         first, second = v[:, 256 * half : 256 * half + 128], v[:, 256 * half + 128 : 256 * half + 256]
         rest = pack_rest(v[:, 512:640], half)
-        for p in range(8 * half, 8 * half + 8):
-            copies[p, 0:128] = first
-            copies[p, 128:256] = second
-            copies[p, 256:320] = rest
+        for p in range(16):
+            if p // 4 % 2 == half:
+                copies[p, 0:128] = first
+                copies[p, 128:256] = second
+                copies[p, 256:320] = rest
 
 
 def first_pack(place, x):
@@ -76,22 +77,69 @@
         in_specs=[SMEM, ANY],
         out_specs=VMEM,
         scratch_shapes=[pltpu.VMEM((ROWS, 128), BF16), pltpu.SemaphoreType.DMA((3,))],
-        compiler_params=pltpu.CompilerParams(vmem_limit_bytes=8 * 2**20),
+        compiler_params=pltpu.CompilerParams(vmem_limit_bytes=4 * 2**20),
         cost_estimate=pl.CostEstimate(flops=2_000_000, bytes_accessed=2_000_000, transcendentals=0),
         name="first_pack",
     )(place, x)
 
 
-def lag_pack(lags):
+def lag_pack(lags, flops=2_000_000):
     return pl.pallas_call(
         lag_pack_kernel,
         out_shape=jax.ShapeDtypeStruct((16, 320, 128), BF16),
         in_specs=[VMEM],
         out_specs=VMEM,
-        compiler_params=pltpu.CompilerParams(vmem_limit_bytes=8 * 2**20),
-        cost_estimate=pl.CostEstimate(flops=2_000_000, bytes_accessed=1_500_000, transcendentals=0),
+        compiler_params=pltpu.CompilerParams(vmem_limit_bytes=4 * 2**20),
+        cost_estimate=pl.CostEstimate(flops=flops, bytes_accessed=1_500_000, transcendentals=0),
         name="lag_pack",
     )(lags)
+
+
+def pack_half(v, upper):
+    return [
+        jnp.where(upper, v[:, 256:384], v[:, 0:128]),
+        jnp.where(upper, v[:, 384:512], v[:, 128:256]),
+        jnp.where(upper, pack_rest(v[:, 512:640], 1), pack_rest(v[:, 512:640], 0)),
+    ]
+
+
+def both_heads(place, x, got):
+    rest = got[2 * ROWS : 2 * ROWS + RIM]
+    theirs = [
+        got[0:RIM],
+        got[ROWS : ROWS + RIM],
+        jnp.where(low_lanes(), rest[0 : RIM // 2], swap(rest[RIM // 2 :])),
+    ]
+    upper = place[1] == 1
+    mine = pack_half(x, upper)
+    even = [jnp.where(upper, b, a) for a, b in zip(mine, theirs)]
+    odd = [jnp.where(upper, a, b) for a, b in zip(mine, theirs)]
+    return even, odd
+
+
+def head_kernel(x, low, high, rows, sem):
+    move = pltpu.make_async_copy(x.at[pl.ds(0, RIM)], rows, sem.at[0])
+    move.start()
+    move.wait()
+    v = rows[...]
+    for half, out in enumerate((low, high)):
+        out[0:RIM] = v[:, 256 * half : 256 * half + 128]
+        out[RIM : 2 * RIM] = v[:, 256 * half + 128 : 256 * half + 256]
+        out[2 * RIM :] = pack_rest(v[:, 512:640], half)
+
+
+def heads(x):
+    one = jax.ShapeDtypeStruct((RIM * 5 // 2, 128), BF16)
+    return pl.pallas_call(
+        head_kernel,
+        out_shape=(one, one),
+        in_specs=[ANY],
+        out_specs=(VMEM, VMEM),
+        scratch_shapes=[pltpu.VMEM((RIM, 640), BF16), pltpu.SemaphoreType.DMA((1,))],
+        compiler_params=pltpu.CompilerParams(vmem_limit_bytes=4 * 2**20),
+        cost_estimate=pl.CostEstimate(flops=2_000_000, bytes_accessed=700_000, transcendentals=0),
+        name="heads",
+    )(x)
 
 
 def lanes_of(half, c):
@@ -136,6 +184,30 @@
     return jnp.sum(jnp.where(lane == 64 + row, te, 0.0), axis=0, keepdims=True)
 
 
+def edge_lags(xm, x2, q, own, oth):
+    parts = []
+    for s, first in ((0, 144), (1, 16)):
+        n = EDGE_USED - first
+        ws, rows = [], []
+        for a in range(4 * s, 4 * s + 4):
+            ws.append(jnp.concatenate([lag_pair(ref, 2 * a, 2 * a + 1) for ref in (own, oth)], axis=0))
+            r = 32 * a + first
+            two = lambda ref, r: jnp.concatenate([ref[b, r : r + n] for b in range(2)], axis=0)
+            rows += [two(xm, r), two(xm, r + 16), two(x2, r)]
+        parts.append(
+            lax.dot_general(
+                jnp.concatenate(rows, axis=1),
+                jnp.concatenate(ws, axis=1),
+                (((1,), (1,)), ((), ())),
+                preferred_element_type=jnp.float32,
+            )
+        )
+    for b in range(2):
+        q[b, 0:16, :] = jnp.zeros((16, 2 * K * SUB), jnp.float32)
+        q[b, 16:144, :] = parts[1][256 * b : 256 * b + 128]
+        q[b, 144:EDGE_USED, :] = parts[1][256 * b + 128 : 256 * b + 256] + parts[0][128 * b : 128 * b + 128]
+
+
 def sum_fine_lags(q, b, span, used, z):
     q[b, used:span, :] = jnp.zeros((span - used, 2 * K * SUB), jnp.float32)
     sums = []
@@ -202,32 +274,30 @@
     return first, second
 
 
-def edge_kernel(place, x, got, own, oth, edges, xm, x2, q, mine, his, sums, sems):
-    z, half = place[0], place[1]
-    first, second = fetch(x, got, half, RIM, RIM, xm, mine, his, sems)
-    for move in first:
-        move.wait()
+def edge_kernel(place, x, got, third, own, oth, edges, xm, x2, q, rows, sem):
+    move = pltpu.make_async_copy(x.at[pl.ds(0, RIM)], rows, sem.at[0])
+    move.start()
     for b in range(2):
         xm[b, 0:RIM] = jnp.zeros((RIM, 256), BF16)
-        if b == 0:
-            v = mine[...]
-            left, right = jnp.where(half == 1, swap(v), v), jnp.where(half == 1, v, swap(v))
-        else:
-            p = his[...]
-            left, right = p, swap(p)
+    move.wait()
+    even, odd = both_heads(place, rows[...], got)
+    turn = place[2] == 1
+    after = [third[0:RIM], third[RIM : 2 * RIM], third[2 * RIM :]]
+    heads = [
+        [jnp.where(turn, n, v) for v, n in zip(even, odd)],
+        [jnp.where(turn, n, v) for v, n in zip(odd, after)],
+    ]
+    for b in range(2):
+        for c in range(2):
+            xm[b, RIM:, 128 * c : 128 * c + 128] = heads[b][c]
+        p = heads[b][2]
+        left, right = jnp.concatenate([p, swap(p)], axis=0), jnp.concatenate([swap(p), p], axis=0)
         lay_out_rest(x2, b, left, right, RIM, 0)
-    for move in second:
-        move.wait()
-    sum_lags(xm, x2, q, own, oth, EDGE_USED, False)
-    for b in range(2):
-        stack = sum_fine_lags(q, b, EDGE_SPAN, EDGE_USED, z)
+    edge_lags(xm, x2, q, own, oth)
+    for b in range(2):
+        stack = sum_fine_lags(q, b, EDGE_SPAN, EDGE_USED, place[0])
         de = window_energy(xm, x2, b, 2 * RIM)
-        store(sums, 4 * b, stack, de, jnp.zeros((1, 128), jnp.float32), 4)
-    low = jnp.where(half == 1, sums[4:8], sums[0:4])
-    high = jnp.where(half == 1, sums[0:4], sums[4:8])
-    turn = place[2] == 1
-    edges[0:4] = jnp.where(turn, high, low)
-    edges[4:8] = jnp.where(turn, jnp.zeros_like(high), high)
+        store(edges, 4 * b, stack, de, jnp.zeros((1, 128), jnp.float32), 4)
 
 
 def main_kernel(place, x, got, own, oth, out, xm, x2, q, mine, his, sems):
@@ -267,11 +337,16 @@
     return pl.pallas_call(
         edge_kernel,
         out_shape=jax.ShapeDtypeStruct((8, 1, 1152), jnp.float32),
-        in_specs=[SMEM, ANY, ANY, VMEM, VMEM],
+        in_specs=[SMEM, ANY, VMEM, VMEM, VMEM, VMEM],
         out_specs=VMEM,
-        scratch_shapes=scratch(RIM, EDGE_SPAN, RIM)
-        + [pltpu.VMEM((8, 1, 1152), jnp.float32), pltpu.SemaphoreType.DMA((6,))],
-        compiler_params=pltpu.CompilerParams(vmem_limit_bytes=20 * 2**20),
+        scratch_shapes=[
+            pltpu.VMEM((2, 2 * RIM, 256), BF16),
+            pltpu.VMEM((2, 2 * RIM, 128), BF16),
+            pltpu.VMEM((2, EDGE_SPAN, 2 * K * SUB), jnp.float32),
+            pltpu.VMEM((RIM, 640), BF16),
+            pltpu.SemaphoreType.DMA((1,)),
+        ],
+        compiler_params=pltpu.CompilerParams(vmem_limit_bytes=10 * 2**20),
         cost_estimate=pl.CostEstimate(flops=1_400_000_000, bytes_accessed=3_200_000, transcendentals=0),
         name="edge_sums",
     )(*args)
@@ -284,7 +359,7 @@
         in_specs=[SMEM, ANY, ANY, VMEM, VMEM],
         out_specs=VMEM,
         scratch_shapes=scratch(ROWS, SPAN, ROWS // 2) + [pltpu.SemaphoreType.DMA((6,))],
-        compiler_params=pltpu.CompilerParams(vmem_limit_bytes=48 * 2**20),
+        compiler_params=pltpu.CompilerParams(vmem_limit_bytes=24 * 2**20),
         cost_estimate=pl.CostEstimate(flops=5_500_000_000, bytes_accessed=5_000_000, transcendentals=0),
         name="main_sums",
     )(*args)
@@ -317,11 +392,11 @@
     tm = lax.axis_size("tm")
     chan = lax.axis_size("chan")
     me = lax.axis_index("tm")
-    half = me // 16
-    turn = jnp.logical_and(lax.rem(me, 8) == 0, lax.rem(me // 8, 2) == 0)
+    half = lax.rem(me // 8, 2)
+    turn = lax.rem(me, 8) == 0
     place = jnp.stack([lax.rem(me, 2), half, turn.astype(jnp.int32)])
     plane = [[2 * i + h for i in range(tm // 2)] for h in range(2)]
-    partner = [(i, i ^ 16) for i in range(tm)]
+    partner = [(i, i ^ 8) for i in range(tm)]
 
     shard = templates.reshape(K * SUB, -1)
     other = lax.ppermute(shard, "tm", [(i, i ^ 1) for i in range(tm)])
@@ -330,17 +405,20 @@
     def exchange(copies):
         return lax.all_to_all(copies, "tm", 0, 0, axis_index_groups=plane)
 
-    own = lax.cond(me // tm == 0, exchange, lambda copies: copies, lag_pack(shard))
-    other, got, own = lax.optimization_barrier((other, got, own))
-    oth = exchange(lag_pack(other))
-
-    edges = edge_sums(place, waveform, got, own, oth)
-    edges = lax.ppermute(edges, "tm", [(i, i - 1 if i % 8 else (i ^ 8) + 7) for i in range(tm)])
+    own = exchange(lag_pack(shard))
+    low, high = heads(waveform)
+    low = lax.ppermute(low, "tm", [(16, 0)])
+    high = lax.ppermute(high, "tm", [(16, 8)])
+    other, got = lax.optimization_barrier((other, got))
+    oth = exchange(lag_pack(other, 100_000_000_000))
+
+    edges = edge_sums(place, waveform, got, low + high, own, oth)
+    edges = lax.ppermute(edges, "tm", [(i, i - 1 if i % 8 else i + 7) for i in range(tm)])
 
     parts = main_sums(place, waveform, got, own, oth)
     edges = jnp.pad(edges.reshape(2, 4, 1, 1152), ((0, 0), (12, 0), (0, 0), (0, 0)))
     parts = parts + edges.reshape(parts.shape)
-    pairs = [[t * chan + c for t in (i, i ^ 16) for c in range(chan)] for i in range(tm // 2)]
+    pairs = [[t * chan + c for t in (i, i ^ 8) for c in range(chan)] for i in range(tm) if i & 8 == 0]
     parts = lax.all_to_all(parts, ("tm", "chan"), 0, 0, axis_index_groups=pairs)
     return finish(parts)
 

time: 117 us -> 113 us (0.966)
  blocking collectives: 66.8 us -> 22.2 us
  waiting for transfers between devices: 0.01 us -> 32.1 us
  starting transfers between devices: 33.1 us -> 38.5 us
  Pallas kernels: 14.6 us -> 16.3 us
    all_to_all x2 -> x0, blocking collectives: 42.7 us -> none  [exchange(): return lax.all_to_all(copies, 'tm', 0, 0, axis_index_groups=plane)]
    all_to_all x0 -> x2, waiting for transfers between devices: none -> 16.5 us  [exchange(): return lax.all_to_all(copies, 'tm', 0, 0, axis_index_groups=plane)]
    ppermute x1 -> x3, waiting for transfers between devices: 0.01 us -> 15.6 us  [the longest x1 15.5 us: local(): low = lax.ppermute(low, 'tm', [(16, 0)])]
    all_to_all x0 -> x2, starting transfers between devices: none -> 10.8 us  [exchange(): return lax.all_to_all(copies, 'tm', 0, 0, axis_index_groups=plane)]
    ppermute x1 -> x3, starting transfers between devices: 12.2 us -> 8.26 us  [the longest x1 6.29 us: local(): lax.ppermute(edges, 'tm', [(i, i - 1 if i % 8 else i + 7) for i in range(...]
    all_to_all x1, blocking collectives: 24.1 us -> 22.2 us  [local(): parts = lax.all_to_all(parts, ('tm', 'chan'), 0, 0, axis_index_groups=pairs)]
    ppermute x1, starting transfers between devices: 5.48 us -> 3.95 us  [local(): got = lax.ppermute(first_pack(place, waveform), 'tm', partner)]
    unnamed x6 -> x8, local copies, waits for them, and re-layouts: 1.33 us -> 2.4 us
  transfers between devices with their start and end apart: 3 -> 7, of which waited for: 0 -> 2; matrix products, arithmetic and copies ran while one was open for 0% -> 0% of each run, Pallas kernels for 8% -> 10%
where the time goes in v6:
time: 113 us; the launch traced here: 112 us
  starting transfers between devices  38.5 us (34%)
  waiting for transfers between devices  32.1 us (28%)
  blocking collectives  22.2 us (20%)
  Pallas kernels  16.3 us (14%)
  local copies, waits for them, and re-layouts  2.48 us (2%)
    all_to_all x1, blocking collectives, local(): parts = lax.all_to_all(parts, ('tm', 'chan'), 0, 0, axis_index_groups=pairs)  22.2 us
    all_to_all x2, waiting for transfers between devices, exchange(): return lax.all_to_all(copies, 'tm', 0, 0, axis_index_groups=plane)  16.5 us
    ppermute x1, waiting for transfers between devices, local(): low = lax.ppermute(low, 'tm', [(16, 0)])  15.5 us
    ppermute x1, starting transfers between devices, local(): other = lax.ppermute(shard, 'tm', [(i, i ^ 1) for i in range(tm)])  15.4 us
    all_to_all x2, starting transfers between devices, exchange(): return lax.all_to_all(copies, 'tm', 0, 0, axis_index_groups=plane)  10.8 us
    pallas_call x1, Pallas kernels, main_sums(): pl.pallas_call(main_kernel, out_shape=jax.ShapeDtypeStruct((32, 1, 1152),...  9.37 us
    ppermute x1, starting transfers between devices, local(): lax.ppermute(edges, 'tm', [(i, i - 1 if i % 8 else i + 7) for i in range(...  6.29 us
    ppermute x1, starting transfers between devices, local(): got = lax.ppermute(first_pack(place, waveform), 'tm', partner)  3.95 us
  transfers between devices with their start and end apart: 7, of which 2 were waited for; matrix products, arithmetic and copies ran while one was open for 0% of the time, Pallas kernels for 10%

profile of v6, /device:TPU:1, one launch (start us, length us, event | category | flops | bytes accessed | tf_op | source)
XLA Modules:
  0.0 112.1 jit_solution(15033363457957787602)
XLA Ops:
  0.0 0.1 pad_add_fusion.place
  0.1 0.0 copy-start
  0.1 1.3 %copy-done = bf16[1024,640]{1,0:T(8,128)(2,1)S(1)} copy-done((bf16[1024,640]{1,0:T(8,128)(2,1)S(1)}, bf16[1024,640]{1,0:T(8,128)(2,1)}, u32[]{:S(2)}) %copy-start) | copy-done | bytes 1310744
  1.4 0.0 copy-start.3
  1.4 0.9 first_pack.1
  2.3 3.9 %collective-permute-start.1 = (bf16[2560,128]{1,0:T(8,128)(2,1)S(1)}, bf16[2560,128]{1,0:T(8,128)(2,1)S(1)}, u32[]{:S(2)}, u32[]{:S(2)}) collective-permute-start(bf16[2560,128]{1,0:T(8,128)(2,1)S(1)} %first_pack.1), channel_id=1, source_target_pairs={{0,128},{16,144},{32,160},{48,176},{64,192},{80,208},{96,224},{112... | collective-permute-start | bytes 1966088 | tf_op jit(solution)/shard_map/ppermute | solution.py:403
  6.2 0.0 copy-done.3
  6.2 15.4 %collective-permute-start = (bf16[128,640]{1,0:T(8,128)(2,1)S(1)}, bf16[128,640]{1,0:T(8,128)(2,1)S(1)}, u32[]{:S(2)}, u32[]{:S(2)}) collective-permute-start(bf16[128,640]{1,0:T(8,128)(2,1)S(1)} %bitcast.7), channel_id=1, source_target_pairs={{0,16},{16,0},{32,48},{48,32},{64,80},{80,64},{96,112},{112,96},{1... | collective-permute-start | bytes 491528 | tf_op jit(solution)/shard_map/ppermute | solution.py:402
  21.7 1.4 %lag_pack.2 = bf16[16,320,128]{2,1,0:T(8,128)(2,1)} custom-call(bf16[128,640]{1,0:T(8,128)(2,1)S(1)} %bitcast.8), custom_call_target="tpu_custom_call" | custom-call | flops 2000000 | bytes 1500000 | tf_op jit(solution)/shard_map/lag_pack/pallas_call | solution.py:87
  23.0 6.5 %all-to-all-start = ((bf16[16,320,128]{2,1,0:T(8,128)(2,1)}), bf16[16,320,128]{2,1,0:T(8,128)(2,1)S(1)}, u32[]{:S(2)}, u32[]{:S(2)}) async-start(bf16[16,320,128]{2,1,0:T(8,128)(2,1)} %lag_pack.2), calls=%async_computation | async-start | bytes 2621440 | tf_op jit(solution)/shard_map/all_to_all | solution.py:406
  29.5 0.0 collective-permute-done.lags
  29.5 0.0 collective-permute-done.1.got
  29.5 0.3 lag_pack.3
  29.8 0.0 copy-start.2
  29.8 1.1 copy-done.2
  30.9 0.0 copy-start.1
  30.9 16.5 %all-to-all-done.own = bf16[16,320,128]{2,1,0:T(8,128)(2,1)S(1)} async-done(((bf16[16,320,128]{2,1,0:T(8,128)(2,1)}), bf16[16,320,128]{2,1,0:T(8,128)(2,1)S(1)}, u32[]{:S(2)}, u32[]{:S(2)}) %all-to-all-start) | async-done | bytes 1310752 | tf_op jit(solution)/shard_map/all_to_all | solution.py:406
  47.5 4.4 %all-to-all-start.1 = ((bf16[16,320,128]{2,1,0:T(8,128)(2,1)}), bf16[16,320,128]{2,1,0:T(8,128)(2,1)}, u32[]{:S(2)}, u32[]{:S(2)}) async-start(bf16[16,320,128]{2,1,0:T(8,128)(2,1)} %copy-done.2), calls=%async_computation.1 | async-start | bytes 2621440 | tf_op jit(solution)/shard_map/all_to_all | solution.py:406
  51.9 0.0 copy-done.1
  51.9 0.2 heads.1
  52.1 1.3 %collective-permute-start.2 = (bf16[640,128]{1,0:T(8,128)(2,1)S(1)}, bf16[640,128]{1,0:T(8,128)(2,1)S(1)}, u32[]{:S(2)}, u32[]{:S(2)}) collective-permute-start(bf16[640,128]{1,0:T(8,128)(2,1)S(1)} %get-tuple-element.11), channel_id=1, source_target_pairs={{256,0},{257,1},{258,2},{259,3},{260,4},{261,5},{262,6},{263,7},{2... | collective-permute-start | bytes 491528 | tf_op jit(solution)/shard_map/ppermute | solution.py:410
  53.4 0.7 collective-permute-start.3
  54.1 15.5 %collective-permute-done.2 = bf16[640,128]{1,0:T(8,128)(2,1)S(1)} collective-permute-done((bf16[640,128]{1,0:T(8,128)(2,1)S(1)}, bf16[640,128]{1,0:T(8,128)(2,1)S(1)}, u32[]{:S(2)}, u32[]{:S(2)}) %collective-permute-start.2) | collective-permute-done | bytes 163872 | tf_op jit(solution)/shard_map/ppermute | solution.py:410
  69.6 0.0 collective-permute-done.3
  69.7 0.0 all-to-all-done.1.oth
  69.7 3.4 %edge_sums.1 = f32[8,1,1152]{2,1,0:T(1,128)S(1)} custom-call(s32[3]{0:T(128)S(1)} %pad_add_fusion.place, bf16[1024,640]{1,0:T(8,128)(2,1)S(1)} %copy-done.1, bf16[2560,128]{1,0:T(8,128)(2,1)S(1)} %collective-permute-done.1.got, bf16[640,128]{1,0:T(8,128)(2,1)S(1)} %add.9.third, bf16[16,320,128]{2,1,0:T(8,128)(2,1)S(1)} %all-to-all-done.own, ...), custom_call_target="tpu_custom_call" | custom-call | flops 1400000000 | bytes 3200000 | tf_op jit(solution)/shard_map/edge_sums/pallas_call | solution.py:337
  73.1 6.3 %collective-permute-start.4 = (f32[8,1,1152]{2,1,0:T(1,128)S(1)}, f32[8,1,1152]{2,1,0:T(1,128)S(1)}, u32[]{:S(2)}, u32[]{:S(2)}) collective-permute-start(f32[8,1,1152]{2,1,0:T(1,128)S(1)} %edge_sums.1), channel_id=1, source_target_pairs={{0,112},{16,0},{32,16},{48,32},{64,48},{80,64},{96,80},{112,96},{1... | collective-permute-start | bytes 110600 | tf_op jit(solution)/shard_map/ppermute | solution.py:416
  79.4 9.4 %main_sums.1 = f32[32,1,1152]{2,1,0:T(1,128)S(1)} custom-call(s32[3]{0:T(128)S(1)} %pad_add_fusion.place, bf16[1024,640]{1,0:T(8,128)(2,1)S(1)} %copy-done.1, bf16[2560,128]{1,0:T(8,128)(2,1)S(1)} %collective-permute-done.1.got, bf16[16,320,128]{2,1,0:T(8,128)(2,1)S(1)} %all-to-all-done.own, bf16[16,320,128]{2,1,0:T(8,128)(2,1)} %all-to-all-done.1.oth), custom_call_target="tpu_custom_call" | custom-call | flops 5500000256 | bytes 5000000 | tf_op jit(solution)/shard_map/main_sums/pallas_call | solution.py:356
  88.7 0.0 collective-permute-done.4
  88.8 0.1 pad.4
  88.8 0.2 bitcast_add_fusion
  89.0 22.2 %all_to_all.15.parts = f32[32,1,1152]{2,1,0:T(1,128)S(1)} all-to-all(f32[32,1,1152]{2,1,0:T(1,128)S(1)} %bitcast_add_fusion), channel_id=1, replica_groups={{0,1,2,3,4,5,6,7,8,9,10,11,12,13,14,15,128,129,130,131,132,133,134,135,..., dimensions={0} | all-to-all | bytes 294912 | tf_op jit(solution)/shard_map/all_to_all | solution.py:422
  111.3 0.8 finish.1
  (1 shorter events, 0.0 us)
Async XLA Ops:
  0.1 1.3 %copy-start = (bf16[1024,640]{1,0:T(8,128)(2,1)S(1)}, bf16[1024,640]{1,0:T(8,128)(2,1)}, u32[]{:S(2)}) copy-start(bf16[1024,640]{1,0:T(8,128)(2,1)} %x.9) | copy-start | bytes 3932164
  1.4 4.8 %copy-start.3 = (bf16[16,8,640]{2,1,0:T(8,128)(2,1)S(1)}, bf16[16,8,640]{2,1,0:T(8,128)(2,1)}, u32[]{:S(2)}) copy-start(bf16[16,8,640]{2,1,0:T(8,128)(2,1)} %param.3) | copy-start | bytes 491524
  2.3 27.3 %collective-permute-start.1 = (bf16[2560,128]{1,0:T(8,128)(2,1)S(1)}, bf16[2560,128]{1,0:T(8,128)(2,1)S(1)}, u32[]{:S(2)}, u32[]{:S(2)}) collective-permute-start(bf16[2560,128]{1,0:T(8,128)(2,1)S(1)} %first_pack.1), channel_id=1, source_target_pairs={{0,128},{16,144},{32,160},{48,176},{64,192},{80,208},{96,224},{112... | collective-permute-start | bytes 1966088 | tf_op jit(solution)/shard_map/ppermute | solution.py:403
  6.2 23.3 %collective-permute-start = (bf16[128,640]{1,0:T(8,128)(2,1)S(1)}, bf16[128,640]{1,0:T(8,128)(2,1)S(1)}, u32[]{:S(2)}, u32[]{:S(2)}) collective-permute-start(bf16[128,640]{1,0:T(8,128)(2,1)S(1)} %bitcast.7), channel_id=1, source_target_pairs={{0,16},{16,0},{32,48},{48,32},{64,80},{80,64},{96,112},{112,96},{1... | collective-permute-start | bytes 491528 | tf_op jit(solution)/shard_map/ppermute | solution.py:402
  23.0 24.4 %all-to-all-start = ((bf16[16,320,128]{2,1,0:T(8,128)(2,1)}), bf16[16,320,128]{2,1,0:T(8,128)(2,1)S(1)}, u32[]{:S(2)}, u32[]{:S(2)}) async-start(bf16[16,320,128]{2,1,0:T(8,128)(2,1)} %lag_pack.2), calls=%async_computation | async-start | bytes 2621440 | tf_op jit(solution)/shard_map/all_to_all | solution.py:406
  29.8 1.1 copy-start.2
  30.9 20.9 %copy-start.1 = (bf16[1024,640]{1,0:T(8,128)(2,1)S(1)}, bf16[1024,640]{1,0:T(8,128)(2,1)}, u32[]{:S(2)}) copy-start(bf16[1024,640]{1,0:T(8,128)(2,1)} %x.9) | copy-start | bytes 3932164
  47.5 22.2 %all-to-all-start.1 = ((bf16[16,320,128]{2,1,0:T(8,128)(2,1)}), bf16[16,320,128]{2,1,0:T(8,128)(2,1)}, u32[]{:S(2)}, u32[]{:S(2)}) async-start(bf16[16,320,128]{2,1,0:T(8,128)(2,1)} %copy-done.2), calls=%async_computation.1 | async-start | bytes 2621440 | tf_op jit(solution)/shard_map/all_to_all | solution.py:406
  52.1 17.5 %collective-permute-start.2 = (bf16[640,128]{1,0:T(8,128)(2,1)S(1)}, bf16[640,128]{1,0:T(8,128)(2,1)S(1)}, u32[]{:S(2)}, u32[]{:S(2)}) collective-permute-start(bf16[640,128]{1,0:T(8,128)(2,1)S(1)} %get-tuple-element.11), channel_id=1, source_target_pairs={{256,0},{257,1},{258,2},{259,3},{260,4},{261,5},{262,6},{263,7},{2... | collective-permute-start | bytes 491528 | tf_op jit(solution)/shard_map/ppermute | solution.py:410
  53.4 16.2 %collective-permute-start.3 = (bf16[640,128]{1,0:T(8,128)(2,1)S(1)}, bf16[640,128]{1,0:T(8,128)(2,1)S(1)}, u32[]{:S(2)}, u32[]{:S(2)}) collective-permute-start(bf16[640,128]{1,0:T(8,128)(2,1)S(1)} %get-tuple-element.12), channel_id=1, source_target_pairs={{256,128},{257,129},{258,130},{259,131},{260,132},{261,133},{262,1... | collective-permute-start | bytes 491528 | tf_op jit(solution)/shard_map/ppermute | solution.py:411
  73.1 15.7 %collective-permute-start.4 = (f32[8,1,1152]{2,1,0:T(1,128)S(1)}, f32[8,1,1152]{2,1,0:T(1,128)S(1)}, u32[]{:S(2)}, u32[]{:S(2)}) collective-permute-start(f32[8,1,1152]{2,1,0:T(1,128)S(1)} %edge_sums.1), channel_id=1, source_target_pairs={{0,112},{16,0},{32,16},{48,32},{64,48},{80,64},{96,80},{112,96},{1... | collective-permute-start | bytes 110600 | tf_op jit(solution)/shard_map/ppermute | solution.py:416

commit v7 on v6

--- a/solution.py
+++ b/solution.py
@@ -115,31 +115,6 @@
     even = [jnp.where(upper, b, a) for a, b in zip(mine, theirs)]
     odd = [jnp.where(upper, a, b) for a, b in zip(mine, theirs)]
     return even, odd
-
-
-def head_kernel(x, low, high, rows, sem):
-    move = pltpu.make_async_copy(x.at[pl.ds(0, RIM)], rows, sem.at[0])
-    move.start()
-    move.wait()
-    v = rows[...]
-    for half, out in enumerate((low, high)):
-        out[0:RIM] = v[:, 256 * half : 256 * half + 128]
-        out[RIM : 2 * RIM] = v[:, 256 * half + 128 : 256 * half + 256]
-        out[2 * RIM :] = pack_rest(v[:, 512:640], half)
-
-
-def heads(x):
-    one = jax.ShapeDtypeStruct((RIM * 5 // 2, 128), BF16)
-    return pl.pallas_call(
-        head_kernel,
-        out_shape=(one, one),
-        in_specs=[ANY],
-        out_specs=(VMEM, VMEM),
-        scratch_shapes=[pltpu.VMEM((RIM, 640), BF16), pltpu.SemaphoreType.DMA((1,))],
-        compiler_params=pltpu.CompilerParams(vmem_limit_bytes=4 * 2**20),
-        cost_estimate=pl.CostEstimate(flops=2_000_000, bytes_accessed=700_000, transcendentals=0),
-        name="heads",
-    )(x)
 
 
 def lanes_of(half, c):
@@ -300,8 +275,10 @@
         store(edges, 4 * b, stack, de, jnp.zeros((1, 128), jnp.float32), 4)
 
 
-def main_kernel(place, x, got, own, oth, out, xm, x2, q, mine, his, sems):
-    z, half = place[0], place[1]
+def layout_kernel(place, x, got, low, high, xm, x2, energy, mine, his, rows, sems):
+    half = place[1]
+    head = pltpu.make_async_copy(x.at[pl.ds(0, RIM)], rows, sems.at[6])
+    head.start()
     first, second = fetch(x, got, half, ROWS, 0, xm, mine, his, sems)
     for move in first:
         move.wait()
@@ -314,23 +291,23 @@
             p = his[...]
             left, right = jnp.concatenate([p, swap(p)], axis=0), jnp.concatenate([swap(p), p], axis=0)
         lay_out_rest(x2, b, left, right, 0, RIM)
+    head.wait()
+    v = rows[...]
+    for h, out in enumerate((low, high)):
+        out[0:RIM] = v[:, 256 * h : 256 * h + 128]
+        out[RIM : 2 * RIM] = v[:, 256 * h + 128 : 256 * h + 256]
+        out[2 * RIM :] = pack_rest(v[:, 512:640], h)
     for move in second:
         move.wait()
+    for b in range(2):
+        energy[b] = window_energy(xm, x2, b, ROWS + RIM)
+
+
+def main_kernel(place, xm, x2, energy, own, oth, out, q):
     te_row = sum_lags(xm, x2, q, own, oth, USED, True)
     for b in range(2):
-        stack = sum_fine_lags(q, b, SPAN, USED, z)
-        de = window_energy(xm, x2, b, ROWS + RIM)
-        store(out, 16 * jnp.where(half == b, 0, 1), stack, de, te_row, 16)
-
-
-def scratch(rows, span, his_rows):
-    return [
-        pltpu.VMEM((2, rows + RIM, 256), BF16),
-        pltpu.VMEM((2, rows + RIM, 128), BF16),
-        pltpu.VMEM((2, span, 2 * K * SUB), jnp.float32),
-        pltpu.VMEM((rows, 128), BF16),
-        pltpu.VMEM((his_rows, 128), BF16),
-    ]
+        stack = sum_fine_lags(q, b, SPAN, USED, place[0])
+        store(out, 16 * jnp.where(place[1] == b, 0, 1), stack, energy[b], te_row, 16)
 
 
 def edge_sums(*args):
@@ -352,13 +329,39 @@
     )(*args)
 
 
+def layout(place, x, got):
+    n = ROWS + RIM
+    one = jax.ShapeDtypeStruct((RIM * 5 // 2, 128), BF16)
+    return pl.pallas_call(
+        layout_kernel,
+        out_shape=(
+            one,
+            one,
+            jax.ShapeDtypeStruct((2, n, 256), BF16),
+            jax.ShapeDtypeStruct((2, n, 128), BF16),
+            jax.ShapeDtypeStruct((2, 8, n), jnp.float32),
+        ),
+        in_specs=[SMEM, ANY, ANY],
+        out_specs=(VMEM,) * 5,
+        scratch_shapes=[
+            pltpu.VMEM((ROWS, 128), BF16),
+            pltpu.VMEM((ROWS // 2, 128), BF16),
+            pltpu.VMEM((RIM, 640), BF16),
+            pltpu.SemaphoreType.DMA((7,)),
+        ],
+        compiler_params=pltpu.CompilerParams(vmem_limit_bytes=12 * 2**20),
+        cost_estimate=pl.CostEstimate(flops=4_000_000, bytes_accessed=4_500_000, transcendentals=0),
+        name="layout",
+    )(place, x, got)
+
+
 def main_sums(*args):
     return pl.pallas_call(
         main_kernel,
         out_shape=jax.ShapeDtypeStruct((32, 1, 1152), jnp.float32),
-        in_specs=[SMEM, ANY, ANY, VMEM, VMEM],
+        in_specs=[SMEM] + [VMEM] * 5,
         out_specs=VMEM,
-        scratch_shapes=scratch(ROWS, SPAN, ROWS // 2) + [pltpu.SemaphoreType.DMA((6,))],
+        scratch_shapes=[pltpu.VMEM((2, SPAN, 2 * K * SUB), jnp.float32)],
         compiler_params=pltpu.CompilerParams(vmem_limit_bytes=24 * 2**20),
         cost_estimate=pl.CostEstimate(flops=5_500_000_000, bytes_accessed=5_000_000, transcendentals=0),
         name="main_sums",
@@ -406,16 +409,16 @@
         return lax.all_to_all(copies, "tm", 0, 0, axis_index_groups=plane)
 
     own = exchange(lag_pack(shard))
-    low, high = heads(waveform)
+    other, got = lax.optimization_barrier((other, got))
+    low, high, *rows = layout(place, waveform, got)
     low = lax.ppermute(low, "tm", [(16, 0)])
     high = lax.ppermute(high, "tm", [(16, 8)])
-    other, got = lax.optimization_barrier((other, got))
     oth = exchange(lag_pack(other, 100_000_000_000))
 
     edges = edge_sums(place, waveform, got, low + high, own, oth)
     edges = lax.ppermute(edges, "tm", [(i, i - 1 if i % 8 else i + 7) for i in range(tm)])
 
-    parts = main_sums(place, waveform, got, own, oth)
+    parts = main_sums(place, *rows, own, oth)
     edges = jnp.pad(edges.reshape(2, 4, 1, 1152), ((0, 0), (12, 0), (0, 0), (0, 0)))
     parts = parts + edges.reshape(parts.shape)
     pairs = [[t * chan + c for t in (i, i ^ 8) for c in range(chan)] for i in range(tm) if i & 8 == 0]

time: 113 us -> 113 us (level)
  waiting for transfers between devices: 32.1 us -> 27.8 us
  local copies, waits for them, and re-layouts: 2.48 us -> 4.38 us
  Pallas kernels: 16.3 us -> 18.1 us
    ppermute x1, waiting for transfers between devices: 15.5 us -> 11.3 us  [local(): low = lax.ppermute(low, 'tm', [(16, 0)])]
    pallas_call x1, Pallas kernels: 0.23 us -> 2.61 us  [layout(): pl.pallas_call(layout_kernel, out_shape=(one, one, jax.ShapeDtypeStruct((...]
    unnamed x8 -> x16, local copies, waits for them, and re-layouts: 2.4 us -> 4.3 us
  transfers between devices with their start and end apart: 7 -> 7, of which waited for: 2 -> 2; matrix products, arithmetic and copies ran while one was open for 0% -> 0% of each run, Pallas kernels for 10% -> 12%
where the time goes in v7:
time: 113 us; the launch traced here: 112 us
  starting transfers between devices  38.4 us (34%)
  waiting for transfers between devices  27.8 us (25%)
  blocking collectives  23.1 us (20%)
  Pallas kernels  18.1 us (16%)
  local copies, waits for them, and re-layouts  4.38 us (4%)
    all_to_all x1, blocking collectives, local(): parts = lax.all_to_all(parts, ('tm', 'chan'), 0, 0, axis_index_groups=pairs)  23.1 us
    all_to_all x2, waiting for transfers between devices, exchange(): return lax.all_to_all(copies, 'tm', 0, 0, axis_index_groups=plane)  16.5 us
    ppermute x1, starting transfers between devices, local(): other = lax.ppermute(shard, 'tm', [(i, i ^ 1) for i in range(tm)])  15.4 us
    ppermute x1, waiting for transfers between devices, local(): low = lax.ppermute(low, 'tm', [(16, 0)])  11.3 us
    all_to_all x2, starting transfers between devices, exchange(): return lax.all_to_all(copies, 'tm', 0, 0, axis_index_groups=plane)  10.9 us
    pallas_call x1, Pallas kernels, main_sums(): pl.pallas_call(main_kernel, out_shape=jax.ShapeDtypeStruct((32, 1, 1152),...  8.68 us
    ppermute x1, starting transfers between devices, local(): lax.ppermute(edges, 'tm', [(i, i - 1 if i % 8 else i + 7) for i in range(...  6.25 us
    unnamed x16, local copies, waits for them, and re-layouts  4.3 us
  transfers between devices with their start and end apart: 7, of which 2 were waited for; matrix products, arithmetic and copies ran while one was open for 0% of the time, Pallas kernels for 12%

profile of v7, /device:TPU:1, one launch (start us, length us, event | category | flops | bytes accessed | tf_op | source)
XLA Modules:
  0.0 112.4 jit_solution(17769137877852647701)
XLA Ops:
  0.0 0.1 pad_add_fusion.place
  0.1 0.0 copy-start
  0.1 1.3 %copy-done = bf16[1024,640]{1,0:T(8,128)(2,1)S(1)} copy-done((bf16[1024,640]{1,0:T(8,128)(2,1)S(1)}, bf16[1024,640]{1,0:T(8,128)(2,1)}, u32[]{:S(2)}) %copy-start) | copy-done | bytes 1310744
  1.4 0.0 copy-start.3
  1.4 0.9 first_pack.1
  2.3 3.9 %collective-permute-start.1 = (bf16[2560,128]{1,0:T(8,128)(2,1)S(1)}, bf16[2560,128]{1,0:T(8,128)(2,1)S(1)}, u32[]{:S(2)}, u32[]{:S(2)}) collective-permute-start(bf16[2560,128]{1,0:T(8,128)(2,1)S(1)} %first_pack.1), channel_id=1, source_target_pairs={{0,128},{16,144},{32,160},{48,176},{64,192},{80,208},{96,224},{112... | collective-permute-start | bytes 1966088 | tf_op jit(solution)/shard_map/ppermute | solution.py:406
  6.2 0.0 copy-done.3
  6.2 15.4 %collective-permute-start = (bf16[128,640]{1,0:T(8,128)(2,1)S(1)}, bf16[128,640]{1,0:T(8,128)(2,1)S(1)}, u32[]{:S(2)}, u32[]{:S(2)}) collective-permute-start(bf16[128,640]{1,0:T(8,128)(2,1)S(1)} %bitcast.7), channel_id=1, source_target_pairs={{0,16},{16,0},{32,48},{48,32},{64,80},{80,64},{96,112},{112,96},{1... | collective-permute-start | bytes 491528 | tf_op jit(solution)/shard_map/ppermute | solution.py:405
  21.7 1.4 %lag_pack.2 = bf16[16,320,128]{2,1,0:T(8,128)(2,1)} custom-call(bf16[128,640]{1,0:T(8,128)(2,1)S(1)} %bitcast.8), custom_call_target="tpu_custom_call" | custom-call | flops 2000000 | bytes 1500000 | tf_op jit(solution)/shard_map/lag_pack/pallas_call | solution.py:87
  23.1 6.5 %all-to-all-start = ((bf16[16,320,128]{2,1,0:T(8,128)(2,1)}), bf16[16,320,128]{2,1,0:T(8,128)(2,1)S(1)}, u32[]{:S(2)}, u32[]{:S(2)}) async-start(bf16[16,320,128]{2,1,0:T(8,128)(2,1)} %lag_pack.2), calls=%async_computation | async-start | bytes 2621440 | tf_op jit(solution)/shard_map/all_to_all | solution.py:409
  29.5 0.0 collective-permute-done.lags
  29.5 0.0 collective-permute-done.1.got
  29.5 0.3 lag_pack.3
  29.9 0.0 copy-start.2
  29.9 1.1 copy-done.2
  30.9 0.0 copy-start.1
  30.9 16.5 %all-to-all-done.own = bf16[16,320,128]{2,1,0:T(8,128)(2,1)S(1)} async-done(((bf16[16,320,128]{2,1,0:T(8,128)(2,1)}), bf16[16,320,128]{2,1,0:T(8,128)(2,1)S(1)}, u32[]{:S(2)}, u32[]{:S(2)}) %all-to-all-start) | async-done | bytes 1310752 | tf_op jit(solution)/shard_map/all_to_all | solution.py:409
  47.5 4.4 %all-to-all-start.1 = ((bf16[16,320,128]{2,1,0:T(8,128)(2,1)}), bf16[16,320,128]{2,1,0:T(8,128)(2,1)}, u32[]{:S(2)}, u32[]{:S(2)}) async-start(bf16[16,320,128]{2,1,0:T(8,128)(2,1)} %copy-done.2), calls=%async_computation.1 | async-start | bytes 2621440 | tf_op jit(solution)/shard_map/all_to_all | solution.py:409
  51.9 0.0 copy-done.1
  51.9 2.6 %layout.1 = (bf16[640,128]{1,0:T(8,128)(2,1)S(1)}, bf16[640,128]{1,0:T(8,128)(2,1)S(1)}, bf16[2,1280,256]{2,1,0:T(8,128)(2,1)S(1)}, bf16[2,1280,128]{2,1,0:T(8,128)(2,1)S(1)}, f32[2,8,1280]{2,1,0:T(8,128)S(1)}) custom-call(s32[3]{0:T(128)S(1)} %pad_add_fusion.place, bf16[1024,640]{1,0:T(8,128)(2,1)S(1)} %copy-done.1, ...), custom_call_target="tpu_custom_call" | custom-call | flops 4000000 | bytes 4500000 | tf_op jit(solution)/shard_map/layout/pallas_call | solution.py:335
  54.5 0.0 copy-start.4
  54.5 1.1 copy-done.4
  55.6 0.0 copy-start.6
  55.6 0.8 copy-done.6
  56.4 1.3 %collective-permute-start.2 = (bf16[640,128]{1,0:T(8,128)(2,1)S(1)}, bf16[640,128]{1,0:T(8,128)(2,1)S(1)}, u32[]{:S(2)}, u32[]{:S(2)}) collective-permute-start(bf16[640,128]{1,0:T(8,128)(2,1)S(1)} %get-tuple-element.17), channel_id=1, source_target_pairs={{256,0},{257,1},{258,2},{259,3},{260,4},{261,5},{262,6},{263,7},{2... | collective-permute-start | bytes 491528 | tf_op jit(solution)/shard_map/ppermute | solution.py:414
  57.7 0.7 collective-permute-start.3
  58.4 11.3 %collective-permute-done.2 = bf16[640,128]{1,0:T(8,128)(2,1)S(1)} collective-permute-done((bf16[640,128]{1,0:T(8,128)(2,1)S(1)}, bf16[640,128]{1,0:T(8,128)(2,1)S(1)}, u32[]{:S(2)}, u32[]{:S(2)}) %collective-permute-start.2) | collective-permute-done | bytes 163872 | tf_op jit(solution)/shard_map/ppermute | solution.py:414
  69.7 0.0 collective-permute-done.3
  69.7 0.0 all-to-all-done.1.oth
  69.7 0.0 copy-start.5
  69.7 0.0 copy-start.7
  69.7 3.5 %edge_sums.1 = f32[8,1,1152]{2,1,0:T(1,128)S(1)} custom-call(s32[3]{0:T(128)S(1)} %pad_add_fusion.place, bf16[1024,640]{1,0:T(8,128)(2,1)S(1)} %copy-done.1, bf16[2560,128]{1,0:T(8,128)(2,1)S(1)} %collective-permute-done.1.got, bf16[640,128]{1,0:T(8,128)(2,1)S(1)} %add.9.third, bf16[16,320,128]{2,1,0:T(8,128)(2,1)S(1)} %all-to-all-done.own, ...), custom_call_target="tpu_custom_call" | custom-call | flops 1400000000 | bytes 3200000 | tf_op jit(solution)/shard_map/edge_sums/pallas_call | solution.py:314
  73.2 6.3 %collective-permute-start.4 = (f32[8,1,1152]{2,1,0:T(1,128)S(1)}, f32[8,1,1152]{2,1,0:T(1,128)S(1)}, u32[]{:S(2)}, u32[]{:S(2)}) collective-permute-start(f32[8,1,1152]{2,1,0:T(1,128)S(1)} %edge_sums.1), channel_id=1, source_target_pairs={{0,112},{16,0},{32,16},{48,32},{64,48},{80,64},{96,80},{112,96},{1... | collective-permute-start | bytes 110600 | tf_op jit(solution)/shard_map/ppermute | solution.py:419
  79.5 0.0 copy-done.5
  79.5 0.0 copy-done.7
  79.5 8.7 %main_sums.1 = f32[32,1,1152]{2,1,0:T(1,128)S(1)} custom-call(s32[3]{0:T(128)S(1)} %pad_add_fusion.place, bf16[2,1280,256]{2,1,0:T(8,128)(2,1)S(1)} %copy-done.5, bf16[2,1280,128]{2,1,0:T(8,128)(2,1)S(1)} %copy-done.7, f32[2,8,1280]{2,1,0:T(8,128)S(1)} %get-tuple-element.15.energy, bf16[16,320,128]{2,1,0:T(8,128)(2,1)S(1)} %all-to-all-done.own, ...), custom_call_target="tpu_custom_call" | custom-call | flops 5500000256 | bytes 5000000 | tf_op jit(solution)/shard_map/main_sums/pallas_call | solution.py:359
  88.2 0.0 collective-permute-done.4
  88.2 0.1 pad.4
  88.3 0.2 bitcast_add_fusion
  88.5 23.1 %all_to_all.15.parts = f32[32,1,1152]{2,1,0:T(1,128)S(1)} all-to-all(f32[32,1,1152]{2,1,0:T(1,128)S(1)} %bitcast_add_fusion), channel_id=1, replica_groups={{0,1,2,3,4,5,6,7,8,9,10,11,12,13,14,15,128,129,130,131,132,133,134,135,..., dimensions={0} | all-to-all | bytes 294912 | tf_op jit(solution)/shard_map/all_to_all | solution.py:425
  111.6 0.8 finish.1
  (1 shorter events, 0.0 us)
Async XLA Ops:
  0.1 1.3 %copy-start = (bf16[1024,640]{1,0:T(8,128)(2,1)S(1)}, bf16[1024,640]{1,0:T(8,128)(2,1)}, u32[]{:S(2)}) copy-start(bf16[1024,640]{1,0:T(8,128)(2,1)} %x.7) | copy-start | bytes 3932164
  1.4 4.8 %copy-start.3 = (bf16[16,8,640]{2,1,0:T(8,128)(2,1)S(1)}, bf16[16,8,640]{2,1,0:T(8,128)(2,1)}, u32[]{:S(2)}) copy-start(bf16[16,8,640]{2,1,0:T(8,128)(2,1)} %param.3) | copy-start | bytes 491524
  2.3 27.3 %collective-permute-start.1 = (bf16[2560,128]{1,0:T(8,128)(2,1)S(1)}, bf16[2560,128]{1,0:T(8,128)(2,1)S(1)}, u32[]{:S(2)}, u32[]{:S(2)}) collective-permute-start(bf16[2560,128]{1,0:T(8,128)(2,1)S(1)} %first_pack.1), channel_id=1, source_target_pairs={{0,128},{16,144},{32,160},{48,176},{64,192},{80,208},{96,224},{112... | collective-permute-start | bytes 1966088 | tf_op jit(solution)/shard_map/ppermute | solution.py:406
  6.2 23.3 %collective-permute-start = (bf16[128,640]{1,0:T(8,128)(2,1)S(1)}, bf16[128,640]{1,0:T(8,128)(2,1)S(1)}, u32[]{:S(2)}, u32[]{:S(2)}) collective-permute-start(bf16[128,640]{1,0:T(8,128)(2,1)S(1)} %bitcast.7), channel_id=1, source_target_pairs={{0,16},{16,0},{32,48},{48,32},{64,80},{80,64},{96,112},{112,96},{1... | collective-permute-start | bytes 491528 | tf_op jit(solution)/shard_map/ppermute | solution.py:405
  23.1 24.4 %all-to-all-start = ((bf16[16,320,128]{2,1,0:T(8,128)(2,1)}), bf16[16,320,128]{2,1,0:T(8,128)(2,1)S(1)}, u32[]{:S(2)}, u32[]{:S(2)}) async-start(bf16[16,320,128]{2,1,0:T(8,128)(2,1)} %lag_pack.2), calls=%async_computation | async-start | bytes 2621440 | tf_op jit(solution)/shard_map/all_to_all | solution.py:409
  29.9 1.1 copy-start.2
  30.9 20.9 %copy-start.1 = (bf16[1024,640]{1,0:T(8,128)(2,1)S(1)}, bf16[1024,640]{1,0:T(8,128)(2,1)}, u32[]{:S(2)}) copy-start(bf16[1024,640]{1,0:T(8,128)(2,1)} %x.7) | copy-start | bytes 3932164
  47.5 22.2 %all-to-all-start.1 = ((bf16[16,320,128]{2,1,0:T(8,128)(2,1)}), bf16[16,320,128]{2,1,0:T(8,128)(2,1)}, u32[]{:S(2)}, u32[]{:S(2)}) async-start(bf16[16,320,128]{2,1,0:T(8,128)(2,1)} %copy-done.2), calls=%async_computation.1 | async-start | bytes 2621440 | tf_op jit(solution)/shard_map/all_to_all | solution.py:409
  54.5 1.1 copy-start.4
  55.6 0.8 copy-start.6
  56.4 13.2 %collective-permute-start.2 = (bf16[640,128]{1,0:T(8,128)(2,1)S(1)}, bf16[640,128]{1,0:T(8,128)(2,1)S(1)}, u32[]{:S(2)}, u32[]{:S(2)}) collective-permute-start(bf16[640,128]{1,0:T(8,128)(2,1)S(1)} %get-tuple-element.17), channel_id=1, source_target_pairs={{256,0},{257,1},{258,2},{259,3},{260,4},{261,5},{262,6},{263,7},{2... | collective-permute-start | bytes 491528 | tf_op jit(solution)/shard_map/ppermute | solution.py:414
  57.7 12.0 %collective-permute-start.3 = (bf16[640,128]{1,0:T(8,128)(2,1)S(1)}, bf16[640,128]{1,0:T(8,128)(2,1)S(1)}, u32[]{:S(2)}, u32[]{:S(2)}) collective-permute-start(bf16[640,128]{1,0:T(8,128)(2,1)S(1)} %get-tuple-element.18), channel_id=1, source_target_pairs={{256,128},{257,129},{258,130},{259,131},{260,132},{261,133},{262,1... | collective-permute-start | bytes 491528 | tf_op jit(solution)/shard_map/ppermute | solution.py:415
  69.7 9.8 %copy-start.5 = (bf16[2,1280,256]{2,1,0:T(8,128)(2,1)S(1)}, bf16[2,1280,256]{2,1,0:T(8,128)(2,1)}, u32[]{:S(2)}) copy-start(bf16[2,1280,256]{2,1,0:T(8,128)(2,1)} %copy-done.4) | copy-start | bytes 3932164
  69.7 9.8 %copy-start.7 = (bf16[2,1280,128]{2,1,0:T(8,128)(2,1)S(1)}, bf16[2,1280,128]{2,1,0:T(8,128)(2,1)}, u32[]{:S(2)}) copy-start(bf16[2,1280,128]{2,1,0:T(8,128)(2,1)} %copy-done.6) | copy-start | bytes 1966084
  73.2 15.0 %collective-permute-start.4 = (f32[8,1,1152]{2,1,0:T(1,128)S(1)}, f32[8,1,1152]{2,1,0:T(1,128)S(1)}, u32[]{:S(2)}, u32[]{:S(2)}) collective-permute-start(f32[8,1,1152]{2,1,0:T(1,128)S(1)} %edge_sums.1), channel_id=1, source_target_pairs={{0,112},{16,0},{32,16},{48,32},{64,48},{80,64},{96,80},{112,96},{1... | collective-permute-start | bytes 110600 | tf_op jit(solution)/shard_map/ppermute | solution.py:419

commit v8 on v7

--- a/solution.py
+++ b/solution.py
@@ -350,7 +350,7 @@
             pltpu.SemaphoreType.DMA((7,)),
         ],
         compiler_params=pltpu.CompilerParams(vmem_limit_bytes=12 * 2**20),
-        cost_estimate=pl.CostEstimate(flops=4_000_000, bytes_accessed=4_500_000, transcendentals=0),
+        cost_estimate=pl.CostEstimate(flops=3_000_000_000, bytes_accessed=4_500_000, transcendentals=0),
         name="layout",
     )(place, x, got)
 

time: 113 us -> 113 us (level)
  no operation moved by 1% of the time
where the time goes in v8:
time: 113 us; the launch traced here: 112 us
  starting transfers between devices  38.5 us (34%)
  waiting for transfers between devices  27.8 us (25%)
  blocking collectives  23.1 us (20%)
  Pallas kernels  18.1 us (16%)
  local copies, waits for them, and re-layouts  4.38 us (4%)
    all_to_all x1, blocking collectives, local(): parts = lax.all_to_all(parts, ('tm', 'chan'), 0, 0, axis_index_groups=pairs)  23.1 us
    all_to_all x2, waiting for transfers between devices, exchange(): return lax.all_to_all(copies, 'tm', 0, 0, axis_index_groups=plane)  16.5 us
    ppermute x1, starting transfers between devices, local(): other = lax.ppermute(shard, 'tm', [(i, i ^ 1) for i in range(tm)])  15.4 us
    ppermute x1, waiting for transfers between devices, local(): low = lax.ppermute(low, 'tm', [(16, 0)])  11.3 us
    all_to_all x2, starting transfers between devices, exchange(): return lax.all_to_all(copies, 'tm', 0, 0, axis_index_groups=plane)  10.9 us
    pallas_call x1, Pallas kernels, main_sums(): pl.pallas_call(main_kernel, out_shape=jax.ShapeDtypeStruct((32, 1, 1152),...  8.68 us
    ppermute x1, starting transfers between devices, local(): lax.ppermute(edges, 'tm', [(i, i - 1 if i % 8 else i + 7) for i in range(...  6.25 us
    unnamed x16, local copies, waits for them, and re-layouts  4.3 us
  transfers between devices with their start and end apart: 7, of which 2 were waited for; matrix products, arithmetic and copies ran while one was open for 0% of the time, Pallas kernels for 12%

profile of v8, /device:TPU:1, one launch (start us, length us, event | category | flops | bytes accessed | tf_op | source)
XLA Modules:
  0.0 112.4 jit_solution(15364378686609445563)
XLA Ops:
  0.0 0.1 pad_add_fusion.place
  0.1 0.0 copy-start
  0.1 1.3 %copy-done = bf16[1024,640]{1,0:T(8,128)(2,1)S(1)} copy-done((bf16[1024,640]{1,0:T(8,128)(2,1)S(1)}, bf16[1024,640]{1,0:T(8,128)(2,1)}, u32[]{:S(2)}) %copy-start) | copy-done | bytes 1310744
  1.4 0.0 copy-start.3
  1.4 0.9 first_pack.1
  2.3 3.9 %collective-permute-start.1 = (bf16[2560,128]{1,0:T(8,128)(2,1)S(1)}, bf16[2560,128]{1,0:T(8,128)(2,1)S(1)}, u32[]{:S(2)}, u32[]{:S(2)}) collective-permute-start(bf16[2560,128]{1,0:T(8,128)(2,1)S(1)} %first_pack.1), channel_id=1, source_target_pairs={{0,128},{16,144},{32,160},{48,176},{64,192},{80,208},{96,224},{112... | collective-permute-start | bytes 1966088 | tf_op jit(solution)/shard_map/ppermute | solution.py:406
  6.2 0.0 copy-done.3
  6.2 15.4 %collective-permute-start = (bf16[128,640]{1,0:T(8,128)(2,1)S(1)}, bf16[128,640]{1,0:T(8,128)(2,1)S(1)}, u32[]{:S(2)}, u32[]{:S(2)}) collective-permute-start(bf16[128,640]{1,0:T(8,128)(2,1)S(1)} %bitcast.7), channel_id=1, source_target_pairs={{0,16},{16,0},{32,48},{48,32},{64,80},{80,64},{96,112},{112,96},{1... | collective-permute-start | bytes 491528 | tf_op jit(solution)/shard_map/ppermute | solution.py:405
  21.7 1.4 %lag_pack.2 = bf16[16,320,128]{2,1,0:T(8,128)(2,1)} custom-call(bf16[128,640]{1,0:T(8,128)(2,1)S(1)} %bitcast.8), custom_call_target="tpu_custom_call" | custom-call | flops 2000000 | bytes 1500000 | tf_op jit(solution)/shard_map/lag_pack/pallas_call | solution.py:87
  23.1 6.5 %all-to-all-start = ((bf16[16,320,128]{2,1,0:T(8,128)(2,1)}), bf16[16,320,128]{2,1,0:T(8,128)(2,1)S(1)}, u32[]{:S(2)}, u32[]{:S(2)}) async-start(bf16[16,320,128]{2,1,0:T(8,128)(2,1)} %lag_pack.2), calls=%async_computation | async-start | bytes 2621440 | tf_op jit(solution)/shard_map/all_to_all | solution.py:409
  29.5 0.0 collective-permute-done.lags
  29.5 0.0 collective-permute-done.1.got
  29.5 0.3 lag_pack.3
  29.9 0.0 copy-start.2
  29.9 1.1 copy-done.2
  30.9 0.0 copy-start.1
  30.9 16.5 %all-to-all-done.own = bf16[16,320,128]{2,1,0:T(8,128)(2,1)S(1)} async-done(((bf16[16,320,128]{2,1,0:T(8,128)(2,1)}), bf16[16,320,128]{2,1,0:T(8,128)(2,1)S(1)}, u32[]{:S(2)}, u32[]{:S(2)}) %all-to-all-start) | async-done | bytes 1310752 | tf_op jit(solution)/shard_map/all_to_all | solution.py:409
  47.5 4.4 %all-to-all-start.1 = ((bf16[16,320,128]{2,1,0:T(8,128)(2,1)}), bf16[16,320,128]{2,1,0:T(8,128)(2,1)}, u32[]{:S(2)}, u32[]{:S(2)}) async-start(bf16[16,320,128]{2,1,0:T(8,128)(2,1)} %copy-done.2), calls=%async_computation.1 | async-start | bytes 2621440 | tf_op jit(solution)/shard_map/all_to_all | solution.py:409
  51.9 0.0 copy-done.1
  51.9 2.6 %layout.1 = (bf16[640,128]{1,0:T(8,128)(2,1)S(1)}, bf16[640,128]{1,0:T(8,128)(2,1)S(1)}, bf16[2,1280,256]{2,1,0:T(8,128)(2,1)S(1)}, bf16[2,1280,128]{2,1,0:T(8,128)(2,1)S(1)}, f32[2,8,1280]{2,1,0:T(8,128)S(1)}) custom-call(s32[3]{0:T(128)S(1)} %pad_add_fusion.place, bf16[1024,640]{1,0:T(8,128)(2,1)S(1)} %copy-done.1, ...), custom_call_target="tpu_custom_call" | custom-call | flops 3000000000 | bytes 4500000 | tf_op jit(solution)/shard_map/layout/pallas_call | solution.py:335
  54.5 0.0 copy-start.4
  54.5 1.1 copy-done.4
  55.6 0.0 copy-start.6
  55.6 0.8 copy-done.6
  56.4 1.3 %collective-permute-start.2 = (bf16[640,128]{1,0:T(8,128)(2,1)S(1)}, bf16[640,128]{1,0:T(8,128)(2,1)S(1)}, u32[]{:S(2)}, u32[]{:S(2)}) collective-permute-start(bf16[640,128]{1,0:T(8,128)(2,1)S(1)} %get-tuple-element.17), channel_id=1, source_target_pairs={{256,0},{257,1},{258,2},{259,3},{260,4},{261,5},{262,6},{263,7},{2... | collective-permute-start | bytes 491528 | tf_op jit(solution)/shard_map/ppermute | solution.py:414
  57.7 0.7 collective-permute-start.3
  58.4 11.3 %collective-permute-done.2 = bf16[640,128]{1,0:T(8,128)(2,1)S(1)} collective-permute-done((bf16[640,128]{1,0:T(8,128)(2,1)S(1)}, bf16[640,128]{1,0:T(8,128)(2,1)S(1)}, u32[]{:S(2)}, u32[]{:S(2)}) %collective-permute-start.2) | collective-permute-done | bytes 163872 | tf_op jit(solution)/shard_map/ppermute | solution.py:414
  69.7 0.0 collective-permute-done.3
  69.7 0.0 all-to-all-done.1.oth
  69.7 0.0 copy-start.5
  69.7 0.0 copy-start.7
  69.7 3.5 %edge_sums.1 = f32[8,1,1152]{2,1,0:T(1,128)S(1)} custom-call(s32[3]{0:T(128)S(1)} %pad_add_fusion.place, bf16[1024,640]{1,0:T(8,128)(2,1)S(1)} %copy-done.1, bf16[2560,128]{1,0:T(8,128)(2,1)S(1)} %collective-permute-done.1.got, bf16[640,128]{1,0:T(8,128)(2,1)S(1)} %add.9.third, bf16[16,320,128]{2,1,0:T(8,128)(2,1)S(1)} %all-to-all-done.own, ...), custom_call_target="tpu_custom_call" | custom-call | flops 1400000000 | bytes 3200000 | tf_op jit(solution)/shard_map/edge_sums/pallas_call | solution.py:314
  73.2 6.3 %collective-permute-start.4 = (f32[8,1,1152]{2,1,0:T(1,128)S(1)}, f32[8,1,1152]{2,1,0:T(1,128)S(1)}, u32[]{:S(2)}, u32[]{:S(2)}) collective-permute-start(f32[8,1,1152]{2,1,0:T(1,128)S(1)} %edge_sums.1), channel_id=1, source_target_pairs={{0,112},{16,0},{32,16},{48,32},{64,48},{80,64},{96,80},{112,96},{1... | collective-permute-start | bytes 110600 | tf_op jit(solution)/shard_map/ppermute | solution.py:419
  79.5 0.0 copy-done.5
  79.5 0.0 copy-done.7
  79.5 8.7 %main_sums.1 = f32[32,1,1152]{2,1,0:T(1,128)S(1)} custom-call(s32[3]{0:T(128)S(1)} %pad_add_fusion.place, bf16[2,1280,256]{2,1,0:T(8,128)(2,1)S(1)} %copy-done.5, bf16[2,1280,128]{2,1,0:T(8,128)(2,1)S(1)} %copy-done.7, f32[2,8,1280]{2,1,0:T(8,128)S(1)} %get-tuple-element.15.energy, bf16[16,320,128]{2,1,0:T(8,128)(2,1)S(1)} %all-to-all-done.own, ...), custom_call_target="tpu_custom_call" | custom-call | flops 5500000256 | bytes 5000000 | tf_op jit(solution)/shard_map/main_sums/pallas_call | solution.py:359
  88.2 0.0 collective-permute-done.4
  88.2 0.1 pad.4
  88.3 0.2 bitcast_add_fusion
  88.5 23.1 %all_to_all.15.parts = f32[32,1,1152]{2,1,0:T(1,128)S(1)} all-to-all(f32[32,1,1152]{2,1,0:T(1,128)S(1)} %bitcast_add_fusion), channel_id=1, replica_groups={{0,1,2,3,4,5,6,7,8,9,10,11,12,13,14,15,128,129,130,131,132,133,134,135,..., dimensions={0} | all-to-all | bytes 294912 | tf_op jit(solution)/shard_map/all_to_all | solution.py:425
  111.6 0.8 finish.1
  (1 shorter events, 0.0 us)
Async XLA Ops:
  0.1 1.3 %copy-start = (bf16[1024,640]{1,0:T(8,128)(2,1)S(1)}, bf16[1024,640]{1,0:T(8,128)(2,1)}, u32[]{:S(2)}) copy-start(bf16[1024,640]{1,0:T(8,128)(2,1)} %x.7) | copy-start | bytes 3932164
  1.4 4.8 %copy-start.3 = (bf16[16,8,640]{2,1,0:T(8,128)(2,1)S(1)}, bf16[16,8,640]{2,1,0:T(8,128)(2,1)}, u32[]{:S(2)}) copy-start(bf16[16,8,640]{2,1,0:T(8,128)(2,1)} %param.3) | copy-start | bytes 491524
  2.3 27.3 %collective-permute-start.1 = (bf16[2560,128]{1,0:T(8,128)(2,1)S(1)}, bf16[2560,128]{1,0:T(8,128)(2,1)S(1)}, u32[]{:S(2)}, u32[]{:S(2)}) collective-permute-start(bf16[2560,128]{1,0:T(8,128)(2,1)S(1)} %first_pack.1), channel_id=1, source_target_pairs={{0,128},{16,144},{32,160},{48,176},{64,192},{80,208},{96,224},{112... | collective-permute-start | bytes 1966088 | tf_op jit(solution)/shard_map/ppermute | solution.py:406
  6.2 23.3 %collective-permute-start = (bf16[128,640]{1,0:T(8,128)(2,1)S(1)}, bf16[128,640]{1,0:T(8,128)(2,1)S(1)}, u32[]{:S(2)}, u32[]{:S(2)}) collective-permute-start(bf16[128,640]{1,0:T(8,128)(2,1)S(1)} %bitcast.7), channel_id=1, source_target_pairs={{0,16},{16,0},{32,48},{48,32},{64,80},{80,64},{96,112},{112,96},{1... | collective-permute-start | bytes 491528 | tf_op jit(solution)/shard_map/ppermute | solution.py:405
  23.1 24.4 %all-to-all-start = ((bf16[16,320,128]{2,1,0:T(8,128)(2,1)}), bf16[16,320,128]{2,1,0:T(8,128)(2,1)S(1)}, u32[]{:S(2)}, u32[]{:S(2)}) async-start(bf16[16,320,128]{2,1,0:T(8,128)(2,1)} %lag_pack.2), calls=%async_computation | async-start | bytes 2621440 | tf_op jit(solution)/shard_map/all_to_all | solution.py:409
  29.9 1.1 copy-start.2
  30.9 20.9 %copy-start.1 = (bf16[1024,640]{1,0:T(8,128)(2,1)S(1)}, bf16[1024,640]{1,0:T(8,128)(2,1)}, u32[]{:S(2)}) copy-start(bf16[1024,640]{1,0:T(8,128)(2,1)} %x.7) | copy-start | bytes 3932164
  47.5 22.2 %all-to-all-start.1 = ((bf16[16,320,128]{2,1,0:T(8,128)(2,1)}), bf16[16,320,128]{2,1,0:T(8,128)(2,1)}, u32[]{:S(2)}, u32[]{:S(2)}) async-start(bf16[16,320,128]{2,1,0:T(8,128)(2,1)} %copy-done.2), calls=%async_computation.1 | async-start | bytes 2621440 | tf_op jit(solution)/shard_map/all_to_all | solution.py:409
  54.5 1.1 copy-start.4
  55.6 0.8 copy-start.6
  56.4 13.2 %collective-permute-start.2 = (bf16[640,128]{1,0:T(8,128)(2,1)S(1)}, bf16[640,128]{1,0:T(8,128)(2,1)S(1)}, u32[]{:S(2)}, u32[]{:S(2)}) collective-permute-start(bf16[640,128]{1,0:T(8,128)(2,1)S(1)} %get-tuple-element.17), channel_id=1, source_target_pairs={{256,0},{257,1},{258,2},{259,3},{260,4},{261,5},{262,6},{263,7},{2... | collective-permute-start | bytes 491528 | tf_op jit(solution)/shard_map/ppermute | solution.py:414
  57.7 12.0 %collective-permute-start.3 = (bf16[640,128]{1,0:T(8,128)(2,1)S(1)}, bf16[640,128]{1,0:T(8,128)(2,1)S(1)}, u32[]{:S(2)}, u32[]{:S(2)}) collective-permute-start(bf16[640,128]{1,0:T(8,128)(2,1)S(1)} %get-tuple-element.18), channel_id=1, source_target_pairs={{256,128},{257,129},{258,130},{259,131},{260,132},{261,133},{262,1... | collective-permute-start | bytes 491528 | tf_op jit(solution)/shard_map/ppermute | solution.py:415
  69.7 9.8 %copy-start.5 = (bf16[2,1280,256]{2,1,0:T(8,128)(2,1)S(1)}, bf16[2,1280,256]{2,1,0:T(8,128)(2,1)}, u32[]{:S(2)}) copy-start(bf16[2,1280,256]{2,1,0:T(8,128)(2,1)} %copy-done.4) | copy-start | bytes 3932164
  69.7 9.8 %copy-start.7 = (bf16[2,1280,128]{2,1,0:T(8,128)(2,1)S(1)}, bf16[2,1280,128]{2,1,0:T(8,128)(2,1)}, u32[]{:S(2)}) copy-start(bf16[2,1280,128]{2,1,0:T(8,128)(2,1)} %copy-done.6) | copy-start | bytes 1966084
  73.2 15.0 %collective-permute-start.4 = (f32[8,1,1152]{2,1,0:T(1,128)S(1)}, f32[8,1,1152]{2,1,0:T(1,128)S(1)}, u32[]{:S(2)}, u32[]{:S(2)}) collective-permute-start(f32[8,1,1152]{2,1,0:T(1,128)S(1)} %edge_sums.1), channel_id=1, source_target_pairs={{0,112},{16,0},{32,16},{48,32},{64,48},{80,64},{96,80},{112,96},{1... | collective-permute-start | bytes 110600 | tf_op jit(solution)/shard_map/ppermute | solution.py:419
